TPU v7x, 32 devices: a whole 2x2x4 slice. The times are simulated.
32 devices in a mesh: dp: 8 (over z, x), psg: 4 (over y, core).
Axes of the slice: x: 2, y: 2, z: 4, core: 2. Of those that a mesh axis runs over, the one named last changes fastest.
Arguments:
- passage_states: bfloat16 [64, 512, 768], P(('dp', 'psg')), may hold values from -6 to 6
- segment_ids: int32 [64, 512], P(('dp', 'psg')), may hold values from 0 to 2, never falling along the last dimension, each value on 1 to 180 neighbouring positions
- query_states: bfloat16 [128, 32, 768], P(('dp', 'psg')), may hold values from -6 to 6
- teacher_scores: float32 [128, 24], P('dp', 'psg'), may hold values from -18 to 18
- w_qkv: bfloat16 [768, 2304], replicated, may hold values from -0.21875 to 0.21875
- bias_q: float32 [768], replicated, may hold values from -1.5 to 1.5
- bias_v: float32 [768], replicated, may hold values from -1.5 to 1.5
- w_out: bfloat16 [768, 768], replicated, may hold values from -1.75 to 1.75
- bias_out: float32 [768], replicated, may hold values from -1.5 to 1.5
- ln1_gain: float32 [768], replicated, may hold values from 0.5 to 1.5
- ln1_bias: float32 [768], replicated, may hold values from -1.5 to 1.5
- w_up: bfloat16 [768, 3072], replicated, may hold values from -0.21875 to 0.21875
- bias_up: float32 [3072], replicated, may hold values from -1.5 to 1.5
- w_down: bfloat16 [3072, 768], replicated, may hold values from -0.109375 to 0.109375
- bias_down: float32 [768], replicated, may hold values from -1.5 to 1.5
- ln2_gain: float32 [768], replicated, may hold values from 0.5 to 1.5
- ln2_bias: float32 [768], replicated, may hold values from -1.5 to 1.5
- w_proj: bfloat16 [768, 128], replicated, may hold values from -0.21875 to 0.21875
Outputs:
- passage_embed: bfloat16 [64, 512, 128], P(('dp', 'psg'))
- query_embed: bfloat16 [128, 32, 128], P(('dp', 'psg'))
- loss: float32 [], replicated
- grad_passages: float32 [64, 512, 768], P(('dp', 'psg'))
- grad_queries: float32 [128, 32, 768], P(('dp', 'psg'))
- grad_w_qkv: float32 [768, 2304], P(('dp', 'psg'))
- grad_bias_q: float32 [768], P(('dp', 'psg'))
- grad_bias_v: float32 [768], P(('dp', 'psg'))
- grad_w_out: float32 [768, 768], P(('dp', 'psg'))
- grad_bias_out: float32 [768], P(('dp', 'psg'))
- grad_ln1_gain: float32 [768], P(('dp', 'psg'))
- grad_ln1_bias: float32 [768], P(('dp', 'psg'))
- grad_w_up: float32 [768, 3072], P(('dp', 'psg'))
- grad_bias_up: float32 [3072], P(('dp', 'psg'))
- grad_w_down: float32 [3072, 768], P(('dp', 'psg'))
- grad_bias_down: float32 [768], P(('dp', 'psg'))
- grad_ln2_gain: float32 [768], P(('dp', 'psg'))
- grad_ln2_bias: float32 [768], P(('dp', 'psg'))
- grad_w_proj: float32 [768, 128], P(('dp', 'psg'))
Inputs may be any that keep to these rules, and one draw needn't show every extreme that they name: `segment_ids`: in each row the passage numbers 0 to 2 follow in order, each passage 1 to 180 positions long, one of them exactly 180.
All inputs are finite; a program needn't handle non-finite values.
Results may differ from a plain program's by a relative error of at most 0.015.
Values may be sent and summed in bfloat16 or wider, within the bound.
A program may use at most 256 MiB of HBM per device.

v0:
```python
import jax
import jax.numpy as jnp
from jax import lax
from jax.sharding import PartitionSpec as P

H = 12
HD = 64
SEGS = 3


largest_score = lax.Precision.HIGHEST
sharpness_divisor = 0.1
root_half = 0.7071067811865476
normal_peak = 0.3989422804014327


def gelu(values):
    return 0.5 * values * (1.0 + jax.scipy.special.erf(values * root_half))


def gelu_slope(values):
    return (
        0.5 * (1.0 + jax.scipy.special.erf(values * root_half))
        + values * jnp.exp(-0.5 * values * values) * normal_peak
    )


def norm_forward(values, gain, shift):
    average = jnp.mean(values, -1, keepdims=True)
    centred = values - average
    inverse_std = lax.rsqrt(jnp.mean(centred * centred, -1, keepdims=True) + 1e-12)
    normed = centred * inverse_std
    return (normed * gain + shift, normed, inverse_std)


def norm_backward(upstream, normed, inverse_std, gain):
    scaled = upstream * gain
    result = inverse_std * (
        scaled
        - jnp.mean(scaled, -1, keepdims=True)
        - normed * jnp.mean(scaled * normed, -1, keepdims=True)
    )
    return (result, jnp.sum(upstream * normed, axis=(0, 1)), jnp.sum(upstream, axis=(0, 1)))


def log_norm(values):
    top = jnp.max(values, -1, keepdims=True)
    shifted = values - top
    return shifted - jnp.log(jnp.sum(jnp.exp(shifted), -1, keepdims=True))


def split_heads(mixed_b, width):
    batch, length = (mixed_b.shape[0], mixed_b.shape[1])
    query_h = mixed_b[..., :width].reshape(batch, length, H, HD)
    key_h = mixed_b[..., width : 2 * width].reshape(batch, length, H, HD)
    content_headwise = mixed_b[..., 2 * width :].reshape(batch, length, H, HD)
    return (query_h, key_h, content_headwise)


def encode(states, segments, params):
    (
        w_qkv,
        bias_mixed,
        w_out,
        bias_out,
        ln1_gain,
        ln1_bias,
        w_up,
        bias_up,
        w_down,
        bias_down,
        ln2_gain,
        ln2_bias,
        w_proj,
    ) = params
    batch, length, width = states.shape
    mixed = (
        jnp.einsum("bld,de->ble", states, w_qkv, preferred_element_type=jnp.float32) + bias_mixed
    )
    mixed_b = mixed.astype(jnp.bfloat16)
    query_h, key_h, content_headwise = split_heads(mixed_b, width)
    scores = (
        jnp.einsum("bqhe,bkhe->bhqk", query_h, key_h, preferred_element_type=jnp.float32) * 0.125
    )
    same_seg = (segments[:, :, None] == segments[:, None, :])[:, None]
    masked = jnp.where(same_seg, scores, -1e30)
    top = jnp.max(masked, -1, keepdims=True)
    power_entries = jnp.exp(masked - top)
    total = jnp.sum(power_entries, -1, keepdims=True)
    log_total = top + jnp.log(total)
    probs_b = (power_entries / total).astype(jnp.bfloat16)
    context = jnp.einsum(
        "bhqk,bkhe->bqhe", probs_b, content_headwise, preferred_element_type=jnp.float32
    )
    context_b = context.reshape(batch, length, width).astype(jnp.bfloat16)
    attended = (
        jnp.einsum("bld,de->ble", context_b, w_out, preferred_element_type=jnp.float32) + bias_out
    )
    first, normed_one, inverse_one = norm_forward(
        states.astype(jnp.float32) + attended, ln1_gain, ln1_bias
    )
    first_b = first.astype(jnp.bfloat16)
    hidden_pre = (
        jnp.einsum("bld,df->blf", first_b, w_up, preferred_element_type=jnp.float32) + bias_up
    )
    hidden_b = gelu(hidden_pre).astype(jnp.bfloat16)
    branch = (
        jnp.einsum("blf,fd->bld", hidden_b, w_down, preferred_element_type=jnp.float32) + bias_down
    )
    second, normed_two, inverse_two = norm_forward(first + branch, ln2_gain, ln2_bias)
    second_b = second.astype(jnp.bfloat16)
    project = jnp.einsum("bld,de->ble", second_b, w_proj, preferred_element_type=jnp.float32)
    inverse_len = lax.rsqrt(jnp.sum(project * project, -1, keepdims=True) + 1e-06)
    unit = project * inverse_len
    kept = (
        states,
        same_seg,
        mixed_b,
        log_total,
        context_b,
        normed_one,
        inverse_one,
        first_b,
        hidden_pre,
        hidden_b,
        normed_two,
        inverse_two,
        second_b,
        unit,
        inverse_len,
    )
    return (unit.astype(jnp.bfloat16), kept)


def encode_back(grad_unit, kept, params):
    (
        w_qkv,
        bias_mixed,
        w_out,
        bias_out,
        ln1_gain,
        ln1_bias,
        w_up,
        bias_up,
        w_down,
        bias_down,
        ln2_gain,
        ln2_bias,
        w_proj,
    ) = params
    (
        states,
        same_seg,
        mixed_b,
        log_total,
        context_b,
        normed_one,
        inverse_one,
        first_b,
        hidden_pre,
        hidden_b,
        normed_two,
        inverse_two,
        second_b,
        unit,
        inverse_len,
    ) = kept
    batch, length, width = states.shape
    grad_project = (
        inverse_len * (grad_unit - unit * jnp.sum(grad_unit * unit, -1, keepdims=True))
    ).astype(jnp.bfloat16)
    g_proj = jnp.einsum("bld,ble->de", second_b, grad_project, preferred_element_type=jnp.float32)
    grad_second = jnp.einsum(
        "ble,de->bld", grad_project, w_proj, preferred_element_type=jnp.float32
    )
    grad_sum_two, g_ln2_gain, g_ln2_bias = norm_backward(
        grad_second, normed_two, inverse_two, ln2_gain
    )
    grad_branch = grad_sum_two.astype(jnp.bfloat16)
    g_down = jnp.einsum("blf,bld->fd", hidden_b, grad_branch, preferred_element_type=jnp.float32)
    g_bias_down = jnp.sum(grad_branch.astype(jnp.float32), axis=(0, 1))
    grad_hidden = jnp.einsum(
        "bld,fd->blf", grad_branch, w_down, preferred_element_type=jnp.float32
    ) * gelu_slope(hidden_pre)
    grad_hidden_b = grad_hidden.astype(jnp.bfloat16)
    g_up = jnp.einsum("bld,blf->df", first_b, grad_hidden_b, preferred_element_type=jnp.float32)
    g_bias_up = jnp.sum(grad_hidden_b.astype(jnp.float32), axis=(0, 1))
    grad_first = grad_sum_two + jnp.einsum(
        "blf,df->bld", grad_hidden_b, w_up, preferred_element_type=jnp.float32
    )
    grad_sum_one, g_ln1_gain, g_ln1_bias = norm_backward(
        grad_first, normed_one, inverse_one, ln1_gain
    )
    grad_attended = grad_sum_one.astype(jnp.bfloat16)
    g_out = jnp.einsum("bld,ble->de", context_b, grad_attended, preferred_element_type=jnp.float32)
    g_bias_out = jnp.sum(grad_attended.astype(jnp.float32), axis=(0, 1))
    grad_context = jnp.einsum(
        "ble,de->bld", grad_attended, w_out, preferred_element_type=jnp.float32
    )
    grad_context = grad_context.astype(jnp.bfloat16).reshape(batch, length, H, HD)
    query_h, key_h, content_headwise = split_heads(mixed_b, width)
    scores = (
        jnp.einsum("bqhe,bkhe->bhqk", query_h, key_h, preferred_element_type=jnp.float32) * 0.125
    )
    probs = jnp.where(same_seg, jnp.exp(scores - log_total), 0.0)
    probs_b = probs.astype(jnp.bfloat16)
    grad_value = jnp.einsum(
        "bhqk,bqhe->bkhe", probs_b, grad_context, preferred_element_type=jnp.float32
    )
    grad_probs = jnp.einsum(
        "bqhe,bkhe->bhqk", grad_context, content_headwise, preferred_element_type=jnp.float32
    )
    grad_scores = (probs * (grad_probs - jnp.sum(probs * grad_probs, -1, keepdims=True))).astype(
        jnp.bfloat16
    )
    grad_query = (
        jnp.einsum("bhqk,bkhe->bqhe", grad_scores, key_h, preferred_element_type=jnp.float32)
        * 0.125
    )
    grad_key = (
        jnp.einsum("bhqk,bqhe->bkhe", grad_scores, query_h, preferred_element_type=jnp.float32)
        * 0.125
    )
    grad_mixed = jnp.concatenate(
        [
            grad_query.reshape(batch, length, width),
            grad_key.reshape(batch, length, width),
            grad_value.reshape(batch, length, width),
        ],
        -1,
    ).astype(jnp.bfloat16)
    g_qkv = jnp.einsum("bld,ble->de", states, grad_mixed, preferred_element_type=jnp.float32)
    g_bias_mixed = jnp.sum(grad_mixed.astype(jnp.float32), axis=(0, 1))
    grad_states = grad_sum_one + jnp.einsum(
        "ble,de->bld", grad_mixed, w_qkv, preferred_element_type=jnp.float32
    )
    grads = (
        g_qkv,
        g_bias_mixed,
        g_out,
        g_bias_out,
        g_ln1_gain,
        g_ln1_bias,
        g_up,
        g_bias_up,
        g_down,
        g_bias_down,
        g_ln2_gain,
        g_ln2_bias,
        g_proj,
    )
    return (grad_states, grads)


def body(
    passage_states,
    segment_ids,
    query_states,
    teacher_scores,
    w_qkv,
    bias_q,
    bias_v,
    w_out,
    bias_out,
    ln1_gain,
    ln1_bias,
    w_up,
    bias_up,
    w_down,
    bias_down,
    ln2_gain,
    ln2_bias,
    w_proj,
):
    width = w_qkv.shape[0]
    emb_width = w_proj.shape[1]
    bias_mixed = jnp.concatenate([bias_q, jnp.zeros_like(bias_q), bias_v])
    params = (
        w_qkv,
        bias_mixed,
        w_out,
        bias_out,
        ln1_gain,
        ln1_bias,
        w_up,
        bias_up,
        w_down,
        bias_down,
        ln2_gain,
        ln2_bias,
        w_proj,
    )
    query_count, query_len = (query_states.shape[0], query_states.shape[1])
    query_block = query_states.reshape(1, query_count * query_len, width)
    query_segments = (jnp.arange(query_count * query_len, dtype=jnp.int32) // query_len)[None]
    query_unit, query_kept = encode(query_block, query_segments, params)
    pass_unit, pass_kept = encode(passage_states, segment_ids, params)
    all_query = lax.all_gather(
        query_unit.reshape(query_count * query_len, emb_width), "psg", axis=0, tiled=True
    )
    flat_pass = pass_unit.reshape(-1, emb_width)
    affinity_entries = lax.dot_general(
        all_query, flat_pass, (((1,), (1,)), ((), ())), preferred_element_type=jnp.float32
    )
    power_entries = jnp.exp((affinity_entries - 1.0) / sharpness_divisor)
    rows_here = segment_ids.shape[0]
    slots = teacher_scores.shape[1]
    passage_index = (jnp.arange(rows_here, dtype=jnp.int32)[:, None] * SEGS + segment_ids).reshape(
        -1
    )
    indicator_matrix = (
        passage_index[:, None] == jnp.arange(slots, dtype=jnp.int32)[None, :]
    ).astype(jnp.float32)
    cumulative_totals = jnp.dot(power_entries, indicator_matrix, precision=largest_score)
    piece_tallies = jnp.sum(indicator_matrix, 0)
    aggregated_lines = jnp.log(cumulative_totals / piece_tallies) + 1.0 / sharpness_divisor
    group_queries = teacher_scores.shape[0]
    logits = jnp.sum(aggregated_lines.reshape(group_queries, -1, slots), 1)
    groups = lax.axis_size("dp")
    all_logits, all_teacher = (
        lax.all_gather(logits, "psg", axis=1, tiled=True),
        lax.all_gather(teacher_scores, "psg", axis=1, tiled=True),
    )
    student = log_norm(all_logits)
    teacher = log_norm(all_teacher)
    group_sum = jnp.sum(jnp.exp(teacher) * (teacher - student))
    full_grad = (jnp.exp(student) - jnp.exp(teacher)) / groups
    grad_logits = lax.dynamic_slice_in_dim(full_grad, lax.axis_index("psg") * slots, slots, 1)
    loss = lax.psum(group_sum / groups, "dp")
    token_count = affinity_entries.shape[0]
    gradient_pooled_rows = jnp.broadcast_to(
        grad_logits[:, None, :], (group_queries, token_count // group_queries, slots)
    ).reshape(token_count, slots)
    grad_sims = (
        jnp.dot(
            gradient_pooled_rows / cumulative_totals, indicator_matrix.T, precision=largest_score
        )
        * power_entries
        / sharpness_divisor
    ).astype(jnp.bfloat16)
    query_part = jnp.dot(grad_sims, flat_pass, preferred_element_type=jnp.float32)
    grad_pass_unit = lax.dot_general(
        grad_sims, all_query, (((0,), (0,)), ((), ())), preferred_element_type=jnp.float32
    )
    grad_query_unit = lax.psum_scatter(
        query_part.astype(jnp.bfloat16), "psg", scatter_dimension=0, tiled=True
    ).astype(jnp.float32)
    grad_pass_states, pass_grads = encode_back(
        grad_pass_unit.reshape(pass_unit.shape), pass_kept, params
    )
    grad_query_states, query_grads = encode_back(
        grad_query_unit.reshape(query_unit.shape), query_kept, params
    )
    totals = jax.tree.map(jnp.add, pass_grads, query_grads)
    (
        g_qkv,
        g_bias_mixed,
        g_out,
        g_bias_out,
        g_ln1_gain,
        g_ln1_bias,
        g_up,
        g_bias_up,
        g_down,
        g_bias_down,
        g_ln2_gain,
        g_ln2_bias,
        g_proj,
    ) = totals
    vectors = jnp.stack(
        [
            g_bias_mixed[:width],
            g_bias_mixed[2 * width :],
            g_bias_out,
            g_ln1_gain,
            g_ln1_bias,
            g_bias_down,
            g_ln2_gain,
            g_ln2_bias,
        ],
        1,
    )
    shards = (
        lax.psum_scatter(g_qkv, ("dp", "psg"), scatter_dimension=0, tiled=True),
        lax.psum_scatter(g_out, ("dp", "psg"), scatter_dimension=0, tiled=True),
        lax.psum_scatter(g_up, ("dp", "psg"), scatter_dimension=0, tiled=True),
        lax.psum_scatter(g_down, ("dp", "psg"), scatter_dimension=0, tiled=True),
        lax.psum_scatter(g_proj, ("dp", "psg"), scatter_dimension=0, tiled=True),
        lax.psum_scatter(vectors, ("dp", "psg"), scatter_dimension=0, tiled=True),
        lax.psum_scatter(g_bias_up, ("dp", "psg"), scatter_dimension=0, tiled=True),
    )
    return (
        pass_unit,
        query_unit.reshape(query_count, query_len, emb_width),
        loss,
        grad_pass_states,
        grad_query_states.reshape(query_count, query_len, width),
        shards[0],
        shards[5][:, 0],
        shards[5][:, 1],
        shards[1],
        shards[5][:, 2],
        shards[5][:, 3],
        shards[5][:, 4],
        shards[2],
        shards[6],
        shards[3],
        shards[5][:, 5],
        shards[5][:, 6],
        shards[5][:, 7],
        shards[4],
    )


def solution(mesh):
    in_specs = (
        P(("dp", "psg"), None, None),
        P(("dp", "psg"), None),
        P(("dp", "psg"), None, None),
        P("dp", "psg"),
        P(),
        P(),
        P(),
        P(),
        P(),
        P(),
        P(),
        P(),
        P(),
        P(),
        P(),
        P(),
        P(),
        P(),
    )
    out_specs = (
        P(("dp", "psg"), None, None),
        P(("dp", "psg"), None, None),
        P(),
        P(("dp", "psg"), None, None),
        P(("dp", "psg"), None, None),
        P(("dp", "psg"), None),
        P(("dp", "psg")),
        P(("dp", "psg")),
        P(("dp", "psg"), None),
        P(("dp", "psg")),
        P(("dp", "psg")),
        P(("dp", "psg")),
        P(("dp", "psg"), None),
        P(("dp", "psg")),
        P(("dp", "psg"), None),
        P(("dp", "psg")),
        P(("dp", "psg")),
        P(("dp", "psg")),
        P(("dp", "psg"), None),
    )
    return jax.shard_map(body, mesh=mesh, in_specs=in_specs, out_specs=out_specs, check_vma=False)
```

profile of v0, /device:TPU:1, one launch (start us, length us, event | category | flops | bytes accessed | tf_op | source)
XLA Modules:
  0.0 914.4 jit_solution(13588484409830347472)
XLA Ops:
  11.4 7.9 all-gather
  41.3 6.1 all_gather.10
  61.6 12.3 %select_reduce_fusion = (f32[2,12,512]{2,1,0:T(8,128)S(1)}, f32[2,12,512,512]{2,3,1,0:T(8,128)}) fusion(pred[2,512,512]{1,2,0:T(8,128)(4,1)} %broadcast_compare_fusion, bf16[2,512,12,64]{1,3,2,0:T(8,128)(2,1)} %bitcast.218, bf16[2,512,12,64]{1,3,2,0:T(8,128)(2,1)} %bitcast.212), kind=kOutput, calls=%fused_computation.6 | convolution fusion | flops 824168448 | bytes 28884992 | tf_op jit(solution)/shard_map/bqhe,bkhe->bhqk/dot_general | solution.py:83
  73.8 11.2 %fusion.1 = f32[2,12,512]{2,1,0:T(8,128)S(1)} fusion(f32[2,12,512,512]{2,3,1,0:T(8,128)} %get-tuple-element.138, f32[2,12,512]{2,1,0:T(8,128)S(1)} %get-tuple-element.137, pred[2,512,512]{1,2,0:T(8,128)(4,1)S(1)} %copy-done.14), kind=kLoop, calls=%fused_computation.7 | loop fusion | flops 25153536 | bytes 25788416 | tf_op jit(solution)/shard_map/reduce_sum | solution.py:89
  85.1 12.2 %fusion.37 = bf16[2,12,64,512]{3,2,1,0:T(8,128)(2,1)S(1)} fusion(bf16[2,512,12,64]{1,3,2,0:T(8,128)(2,1)S(1)} %bitcast.222, f32[2,12,512,512]{2,3,1,0:T(8,128)} %get-tuple-element.138, f32[2,12,512]{2,1,0:T(8,128)S(1)} %fusion.1, f32[2,12,512]{2,1,0:T(8,128)S(1)} %get-tuple-element.137, pred[2,512,512]{1,2,0:T(8,128)(4,1)S(1)} %copy-done.14), kind=kOutput, calls=%fused_computation.73 | convolution fusion | flops 837550080 | bytes 28934144 | tf_op jit(solution)/shard_map/bhqk,bkhe->bqhe/dot_general | solution.py:92
  101.8 9.3 %multiply_convert_fusion.1 = (bf16[2,512,3072]{2,1,0:T(8,128)(2,1)S(1)}, f32[2,512,3072]{2,1,0:T(8,128)}) fusion(f32[3072]{0:T(1024)S(1)} %copy-done.102, bf16[768,3072]{1,0:T(8,128)(2,1)S(1)} %bitcast.215, f32[2,512,768]{2,1,0:T(8,128)S(1)} %get-tuple-element.140, f32[768]{0:T(1024)S(1)} %copy-done.59, f32[768]{0:T(1024)S(1)} %copy-done.50, ...), kind=kOutput, calls=%fused_computation.17 | convolution fusion | flops 4854644736 | bytes 26765312 | tf_op jit(solution)/shard_map/bld,df->blf/dot_general | solution.py:104
  111.1 5.5 fusion.119
  126.6 5.7 all-gather.1
  152.6 11.0 %multiply_reduce_fusion.1 = (f32[768]{0:T(1024)}, f32[2,512]{1,0:T(2,128)}, f32[2,512]{1,0:T(2,128)}, f32[768]{0:T(1024)}, f32[2,512,768]{2,1,0:T(8,128)}) fusion(f32[2,512,768]{2,1,0:T(8,128)} %copy-done.15, f32[2,512]{1,0:T(2,128)} %copy-done.93, f32[2,512]{1,0:T(2,128)} %copy-done.76, f32[768]{0:T(1024)S(1)} %copy-done.67, bf16[768,128]{1,0:T(8,128)(2,1)} %param.35, ...), kind=kOutput, calls=%fused_computation.45 | convolution fusion | flops 209319552 | bytes 7566336 | tf_op jit(solution)/shard_map/ble,de->bld/dot_general | solution.py:173
  168.4 13.0 %convert_reduce_fusion = (f32[3072]{0:T(1024)}, bf16[2,512,3072]{2,1,0:T(8,128)(2,1)S(1)}) fusion(f32[2,512,3072]{2,1,0:T(8,128)} %get-tuple-element.142, f32[3072]{0:T(1024)S(1)} %copy-done.103, bf16[2,512,768]{2,1,0:T(8,128)(2,1)S(1)} %get-tuple-element.116, bf16[3072,768]{1,0:T(8,128)(2,1)} %param.31), kind=kOutput, calls=%fused_computation.16 | convolution fusion | flops 4872729600 | bytes 25190400 | tf_op jit(solution)/shard_map/bld,fd->blf/dot_general | solution.py:182
  181.5 10.8 %multiply_reduce_fusion.2 = (f32[768]{0:T(1024)}, f32[2,512]{1,0:T(2,128)S(1)}, f32[2,512]{1,0:T(2,128)S(1)}, f32[768]{0:T(1024)}, f32[2,512,768]{2,1,0:T(8,128)}) fusion(f32[2,512,768]{2,1,0:T(8,128)S(1)} %copy-done.2, f32[2,512]{1,0:T(2,128)S(1)} %copy-done.69, f32[2,512]{1,0:T(2,128)S(1)} %broadcast_multiply_fusion.5, f32[768]{0:T(1024)S(1)} %copy-done.50, ...), kind=kOutput, calls=%fused_computation.47 | convolution fusion | flops 4845203456 | bytes 23638016 | tf_op jit(solution)/shard_map/blf,df->bld/dot_general | solution.py:188
  203.6 12.4 %fusion.38 = bf16[2,12,64,512]{3,2,1,0:T(8,128)(2,1)} fusion(bf16[2,512,12,64]{1,3,2,0:T(8,128)(2,1)} %bitcast.223, f32[2,12,512,512]{2,3,1,0:T(8,128)} %get-tuple-element.138, f32[2,12,512]{2,1,0:T(8,128)} %log_add_fusion, pred[2,512,512]{1,2,0:T(8,128)(4,1)} %broadcast_compare_fusion), kind=kOutput, calls=%fused_computation.74 | convolution fusion | flops 831258624 | bytes 28884992 | tf_op jit(solution)/shard_map/bhqk,bqhe->bkhe/dot_general | solution.py:207
  216.0 21.7 %multiply_reduce_fusion = (f32[2,12,512]{2,1,0:T(8,128)}, f32[2,12,512,512]{2,3,1,0:T(8,128)}) fusion(f32[2,12,512,512]{2,3,1,0:T(8,128)} %get-tuple-element.138, f32[2,12,512]{2,1,0:T(8,128)} %log_add_fusion, pred[2,512,512]{1,2,0:T(8,128)(4,1)} %broadcast_compare_fusion, bf16[2,512,12,64]{1,3,2,0:T(8,128)(2,1)} %bitcast.224, ...), kind=kOutput, calls=%fused_computation.2 | convolution fusion | flops 836751360 | bytes 54099968 | tf_op jit(solution)/shard_map/bqhe,bkhe->bhqk/dot_general | solution.py:210
  237.6 21.5 %multiply_convert_fusion = bf16[2,12,512,512]{2,3,1,0:T(8,128)(2,1)} fusion(f32[2,12,512,512]{2,3,1,0:T(8,128)} %get-tuple-element.160, f32[2,12,512,512]{2,3,1,0:T(8,128)} %get-tuple-element.138, f32[2,12,512]{2,1,0:T(8,128)} %get-tuple-element.159, f32[2,12,512]{2,1,0:T(8,128)} %log_add_fusion, pred[2,512,512]{1,2,0:T(8,128)(4,1)} %broadcast_compare_fusion), kind=kLoop, calls=%fused_computation.1 | loop fusion | flops 37748736 | bytes 63537152 | tf_op jit(solution)/shard_map/convert_element_type | solution.py:213
  259.2 9.8 %multiply_convert_fusion.2 = bf16[2,12,64,512]{3,2,1,0:T(8,128)(2,1)} fusion(bf16[2,512,12,64]{1,3,2,0:T(8,128)(2,1)S(1)} %bitcast.219, bf16[2,12,512,512]{2,3,1,0:T(8,128)(2,1)} %multiply_convert_fusion), kind=kOutput, calls=%fused_computation.49 | convolution fusion | flops 806879232 | bytes 15728640 | tf_op jit(solution)/shard_map/bhqk,bqhe->bkhe/dot_general | solution.py:221
  269.0 7.9 multiply_convert_fusion.3
  284.7 9.5 %convolution_bitcast_fusion = f32[768,128]{1,0:T(8,128)} fusion(f32[2,512,128]{2,1,0:T(8,128)} %bitcast.256, f32[2,512,128]{2,1,0:T(8,128)} %copy-done.58, f32[2,512]{1,0:T(2,128)} %copy-done.95, f32[2,512,768]{2,1,0:T(8,128)} %copy-done.15, f32[768]{0:T(1024)} %param.34, f32[768]{0:T(1024)S(1)} %copy-done.67, f32[2,512]{1,0:T(2,128)} %copy-done.93, ...), kind=kOutput, calls=%fused_computation.89 | convolution fusion | flops 206177408 | bytes 4605952 | tf_op jit(solution)/shard_map/bld,ble->de/dot_general | solution.py:172
  303.8 5.3 convert_reduce_fusion.4
  318.4 9.8 %fusion.112 = f32[2304,768,1]{1,0,2:T(8,128)} fusion(bf16[2,512,768]{2,1,0:T(8,128)(2,1)} %param.18, bf16[2,512,768]{2,1,0:T(8,128)(2,1)} %copy.135, bf16[2,512,768]{2,1,0:T(8,128)(2,1)} %copy.134, bf16[2,512,768]{2,1,0:T(8,128)(2,1)} %copy.133), kind=kOutput, calls=%fused_computation.230 | convolution fusion | flops 3638034432 | bytes 13369344 | tf_op jit(solution)/shard_map/bld,ble->de/dot_general | solution.py:232
  336.1 7.0 fusion.13
  343.1 8.0 copy.158
  351.8 9.0 fusion.86
  360.9 5.2 bitcast_add_fusion.1
  366.2 8.0 fusion.127
  374.2 5.1 bitcast_add_fusion
  382.0 18.4 %psum.7 = f32[]{:T(128)} all-reduce(f32[]{:T(128)S(6)} %div.118), channel_id=1, replica_groups=mesh['dp'=8,'psg'=4] {'dp'}, use_global_device_ids=true, to_apply=%region_21.22 | all-reduce | flops 1 | bytes 8 | tf_op jit(solution)/shard_map/psum | solution.py:329
  404.4 7.5 fusion.34
  417.8 41.3 %all-reduce.3 = (f32[768,8]{0,1:T(8,128)}, f32[3072]{0:T(1024)}) all-reduce(f32[768,8]{0,1:T(8,128)} %stack.8, f32[3072]{0:T(1024)S(1)} %add.431), channel_id=4, replica_groups=mesh['dp'=8,'psg'=4] {'dp','psg'}, use_global_device_ids=true, to_apply=%region_50.51.clone | all-reduce | flops 9216 | bytes 73728
  464.9 34.1 %reduce-scatter.14.cloned.1.call-done = f32[24,768]{1,0:T(8,128)} async-done(((f32[768,768]{1,0:T(8,128)}), f32[24,768]{1,0:T(8,128)}) %reduce-scatter.14.cloned.1.call-update) | async-done | bytes 73744 | tf_op jit(solution)/shard_map/reduce_scatter | solution.py:385
  499.1 125.2 %reduce-scatter.20.cloned.1.call-done = f32[24,2304]{1,0:T(8,128)} async-done(((f32[768,2304]{1,0:T(8,128)}), f32[24,2304]{1,0:T(8,128)}) %reduce-scatter.20.cloned.1.call-update) | async-done | bytes 221200
  624.3 140.9 %reduce-scatter.16.cloned.1.call-done = f32[24,3072]{1,0:T(8,128)} async-done(((f32[768,3072]{1,0:T(8,128)}), f32[24,3072]{1,0:T(8,128)}) %reduce-scatter.16.cloned.1.call-update) | async-done | bytes 294928 | tf_op jit(solution)/shard_map/reduce_scatter | solution.py:386
  765.2 142.0 %reduce-scatter.18.cloned.1.call-done = f32[96,768]{1,0:T(8,128)} async-done(((f32[3072,768]{1,0:T(8,128)}), f32[96,768]{1,0:T(8,128)}) %reduce-scatter.18.cloned.1.call-update) | async-done | bytes 294928 | tf_op jit(solution)/shard_map/reduce_scatter | solution.py:387
  (409 shorter events, 143.2 us)
Async XLA Ops:
  7.2 15.4 %copy-start = (bf16[768,2304]{1,0:T(8,128)(2,1)S(1)}, bf16[768,2304]{1,0:T(8,128)(2,1)}, u32[]{:S(2)}) copy-start(bf16[768,2304]{1,0:T(8,128)(2,1)} %param.22) | copy-start | bytes 10616836
  7.2 287.0 %reduce-scatter.12.cloned.1.call-start = ((), (), s32[]{:S(2)}) async-start(), calls=%async_computation.6 | async-start | bytes 163840 | tf_op jit(solution)/shard_map/reduce_scatter | solution.py:345
  11.4 20.3 %copy-start.56 = (pred[128,128]{0,1:T(8,128)(4,1)}, pred[128,128]{0,1:T(8,128)(4,1)S(1)}, u32[]{:S(2)}) copy-start(pred[128,128]{0,1:T(8,128)(4,1)S(1)} %broadcast_compare_fusion.1) | copy-start | bytes 49156
  38.9 12.6 %copy-start.106 = (f32[128]{0:T(128)}, f32[128]{0:T(128)S(1)}, u32[]{:S(2)}) copy-start(f32[128]{0:T(128)S(1)} %broadcast_multiply_fusion.10) | copy-start | bytes 1540
  61.6 12.3 %copy-start.14 = (pred[2,512,512]{1,2,0:T(8,128)(4,1)S(1)}, pred[2,512,512]{1,2,0:T(8,128)(4,1)}, u32[]{:S(2)}) copy-start(pred[2,512,512]{1,2,0:T(8,128)(4,1)} %broadcast_compare_fusion) | copy-start | bytes 1572868
  73.8 11.2 %copy-start.19 = (bf16[2,512,768]{1,2,0:T(8,128)(2,1)S(1)}, bf16[2,512,768]{1,2,0:T(8,128)(2,1)}, u32[]{:S(2)}) copy-start(bf16[2,512,768]{1,2,0:T(8,128)(2,1)} %copy.120) | copy-start | bytes 4718596
  85.0 12.3 %copy-start.60 = (f32[2,12,512]{2,1,0:T(8,128)}, f32[2,12,512]{2,1,0:T(8,128)S(1)}, u32[]{:S(2)}) copy-start(f32[2,12,512]{2,1,0:T(8,128)S(1)} %fusion.1) | copy-start | bytes 147460
  85.0 12.3 %copy-start.25 = (bf16[768,768]{1,0:T(8,128)(2,1)S(1)}, bf16[768,768]{1,0:T(8,128)(2,1)}, u32[]{:S(2)}) copy-start(bf16[768,768]{1,0:T(8,128)(2,1)} %param.25) | copy-start | bytes 3538948
  85.1 12.3 %copy-start.110 = (f32[768]{0:T(1024)S(1)}, f32[768]{0:T(1024)}, u32[]{:S(2)}) copy-start(f32[768]{0:T(1024)} %param.26) | copy-start | bytes 9220
  85.1 12.3 %copy-start.123 = (bf16[2,512,768]{2,1,0:T(8,128)(2,1)S(1)}, bf16[2,512,768]{2,1,0:T(8,128)(2,1)}, u32[]{:S(2)}) copy-start(bf16[2,512,768]{2,1,0:T(8,128)(2,1)} %param.18) | copy-start | bytes 4718596
  97.4 13.7 %slice-start.6 = ((s8[4718592]{0:T(1024)(128)(4,1)}), s8[4194304]{0:T(1024)(128)(4,1)S(1)}, s32[]{:S(2)}) async-start(s8[4718592]{0:T(1024)(128)(4,1)} %bitcast.228), calls=%async_computation.18 | async-start | bytes 8388608
  99.1 12.0 %copy-start.1 = (f32[2,512,768]{2,1,0:T(8,128)}, f32[2,512,768]{2,1,0:T(8,128)S(1)}, u32[]{:S(2)}) copy-start(f32[2,512,768]{2,1,0:T(8,128)S(1)} %get-tuple-element.140) | copy-start | bytes 9437188
  99.1 93.2 %copy-start.63 = (f32[2,512]{1,0:T(2,128)}, f32[2,512]{1,0:T(2,128)S(1)}, u32[]{:S(2)}) copy-start(f32[2,512]{1,0:T(2,128)S(1)} %broadcast_multiply_fusion.5) | copy-start | bytes 12292
  148.1 316.8 %reduce-scatter.22.cloned.1.call-start = ((), (), s32[]{:S(2)}) async-start(), calls=%async_computation.11 | async-start | bytes 405504
  164.2 17.2 %slice-start.2 = ((s8[4718592]{0:T(1024)(128)(4,1)}), s8[4194304]{0:T(1024)(128)(4,1)S(1)}, s32[]{:S(2)}) async-start(s8[4718592]{0:T(1024)(128)(4,1)} %bitcast.216), calls=%async_computation.14 | async-start | bytes 8388608
  168.4 13.1 %copy-start.47 = (bf16[2,512,768]{2,1,0:T(8,128)(2,1)}, bf16[2,512,768]{2,1,0:T(8,128)(2,1)S(1)}, u32[]{:S(2)}) copy-start(bf16[2,512,768]{2,1,0:T(8,128)(2,1)S(1)} %get-tuple-element.116) | copy-start | bytes 4718596
  168.4 13.1 %copy-start.2 = (f32[2,512,768]{2,1,0:T(8,128)S(1)}, f32[2,512,768]{2,1,0:T(8,128)}, u32[]{:S(2)}) copy-start(f32[2,512,768]{2,1,0:T(8,128)} %copy-done.1) | copy-start | bytes 9437188
  168.4 13.1 %slice-start.3 = ((s8[4718592]{0:T(1024)(128)(4,1)}), s8[524288]{0:T(1024)(128)(4,1)S(1)}, s32[]{:S(2)}) async-start(s8[4718592]{0:T(1024)(128)(4,1)} %bitcast.216), calls=%async_computation.15 | async-start | bytes 1048576
  168.4 13.1 %copy-start.16 = (f32[2,512,768]{2,1,0:T(8,128)S(1)}, f32[2,512,768]{2,1,0:T(8,128)}, u32[]{:S(2)}) copy-start(f32[2,512,768]{2,1,0:T(8,128)} %copy-done.15) | copy-start | bytes 9437188
  168.4 13.1 %copy-start.69 = (f32[2,512]{1,0:T(2,128)S(1)}, f32[2,512]{1,0:T(2,128)}, u32[]{:S(2)}) copy-start(f32[2,512]{1,0:T(2,128)} %copy-done.68) | copy-start | bytes 12292
  168.4 13.1 %copy-start.77 = (f32[2,512]{1,0:T(2,128)S(1)}, f32[2,512]{1,0:T(2,128)}, u32[]{:S(2)}) copy-start(f32[2,512]{1,0:T(2,128)} %copy-done.76) | copy-start | bytes 12292
  168.4 13.1 %copy-start.94 = (f32[2,512]{1,0:T(2,128)S(1)}, f32[2,512]{1,0:T(2,128)}, u32[]{:S(2)}) copy-start(f32[2,512]{1,0:T(2,128)} %copy-done.93) | copy-start | bytes 12292
  237.6 21.5 %copy-start.11 = (bf16[2,512,768]{1,2,0:T(8,128)(2,1)S(1)}, bf16[2,512,768]{1,2,0:T(8,128)(2,1)}, u32[]{:S(2)}) copy-start(bf16[2,512,768]{1,2,0:T(8,128)(2,1)} %copy.121) | copy-start | bytes 4718596
  301.0 198.1 %reduce-scatter.14.cloned.1.call-start = ((), (), s32[]{:S(2)}) async-start(), calls=%async_computation.7 | async-start | bytes 2433024 | tf_op jit(solution)/shard_map/reduce_scatter | solution.py:385
  317.7 306.7 %reduce-scatter.20.cloned.1.call-start = ((), (), s32[]{:S(2)}) async-start(), calls=%async_computation.10 | async-start | bytes 7299072
  351.2 414.0 %reduce-scatter.16.cloned.1.call-start = ((), (), s32[]{:S(2)}) async-start(), calls=%async_computation.8 | async-start | bytes 9732096 | tf_op jit(solution)/shard_map/reduce_scatter | solution.py:386
  366.1 541.1 %reduce-scatter.18.cloned.1.call-start = ((), (), s32[]{:S(2)}) async-start(), calls=%async_computation.9 | async-start | bytes 9732096 | tf_op jit(solution)/shard_map/reduce_scatter | solution.py:387
  381.4 22.0 %copy-start.65 = (f32[2,512]{1,0:T(2,128)S(1)}, f32[2,512]{1,0:T(2,128)}, u32[]{:S(2)}) copy-start(f32[2,512]{1,0:T(2,128)} %copy-done.63) | copy-start | bytes 12292
  381.4 22.0 %copy-start.71 = (f32[2,512]{1,0:T(2,128)S(1)}, f32[2,512]{1,0:T(2,128)}, u32[]{:S(2)}) copy-start(f32[2,512]{1,0:T(2,128)} %copy-done.68) | copy-start | bytes 12292
  381.4 22.0 %copy-start.90 = (f32[2,512]{1,0:T(2,128)S(1)}, f32[2,512]{1,0:T(2,128)}, u32[]{:S(2)}) copy-start(f32[2,512]{1,0:T(2,128)} %copy-done.89) | copy-start | bytes 12292
  404.4 12.0 %copy-start.104 = (f32[3072]{0:T(1024)S(1)}, f32[3072]{0:T(1024)}, u32[]{:S(2)}) copy-start(f32[3072]{0:T(1024)} %get-tuple-element.165) | copy-start | bytes 36868
  404.4 12.0 %copy-start.105 = (f32[3072]{0:T(1024)S(1)}, f32[3072]{0:T(1024)}, u32[]{:S(2)}) copy-start(f32[3072]{0:T(1024)} %get-tuple-element.167) | copy-start | bytes 36868
  (109 other events, 501.5 us)
Sparse Core Ops, SparseCore 0:
  148.2 19.6 reduce-scatter.11
  301.1 93.4 reduce-scatter.21
  400.5 98.5 reduce-scatter.13
  506.1 118.1 reduce-scatter.19
  630.6 134.4 reduce-scatter.15
  772.5 134.6 reduce-scatter.17
where the time goes:
time: 923 us; the launch traced here: 914 us
  waiting for transfers between devices  442 us (48%)
  matrix products  242 us (26%)
  blocking collectives  79.4 us (9%)
  other arithmetic  69.2 us (7%)
  local copies, waits for them, and re-layouts  64 us (7%)
  between operations  16.7 us (2%)
    reduce_scatter x1, waiting for transfers between devices, body(): lax.psum_scatter(g_down, ('dp', 'psg'), scatter_dimension=0, tiled=True)  142 us
    reduce_scatter x1, waiting for transfers between devices, body(): lax.psum_scatter(g_up, ('dp', 'psg'), scatter_dimension=0, tiled=True)  141 us
    unnamed x8, waiting for transfers between devices  125 us
    unnamed x1, blocking collectives  41.3 us
    reduce_scatter x1, waiting for transfers between devices, body(): lax.psum_scatter(g_out, ('dp', 'psg'), scatter_dimension=0, tiled=True)  34.1 us
    unnamed x276, local copies, waits for them, and re-layouts  26 us
    dot_general x2, matrix products, encode_back(): jnp.einsum('bqhe,bkhe->bhqk', grad_context, content_headwise, preferred_e...  23.5 us
    convert_element_type x2, other arithmetic, encode_back(): (probs * (grad_probs - jnp.sum(probs * grad_probs, -1, keepdims=True))).a...  22.9 us
  transfers between devices with their start and end apart: 6, of which 4 were waited for; matrix products, arithmetic and copies ran while one was open for 27% of the time, Pallas kernels for 0%

commit v1 on v0

v1 whole, which is shorter than its diff:
```python
import functools

import jax
import jax.numpy as jnp
from jax import lax
from jax.experimental import pallas as pl
from jax.experimental.pallas import tpu as pltpu
from jax.sharding import PartitionSpec as P

F32 = jnp.float32
BF = jnp.bfloat16
MESH = pl.DeviceIdType.MESH
H = 12
HD = 64
SEGS = 3
LOG2E = 1.4426950408889634
SHARP = 0.1
TILES = ((0, 0, 256, 0), (128, 0, 384, 256), (256, 128, 384, 640), (384, 256, 256, 1024))
PW = 1280
LEN = 512


def nn(a, b):
    return lax.dot_general(a, b, (((1,), (0,)), ((), ())), preferred_element_type=F32)


def nt(a, b):
    return lax.dot_general(a, b, (((1,), (1,)), ((), ())), preferred_element_type=F32)


def tn(a, b):
    return lax.dot_general(a, b, (((0,), (0,)), ((), ())), preferred_element_type=F32)


def at(i, n):
    return pl.ds(pl.multiple_of(i * n, n), n)


def rows_at(start, n, unit):
    return pl.ds(pl.multiple_of(start, unit), n)


class Space:
    pass


def norm_stats(v):
    mean = jnp.mean(v, -1, keepdims=True)
    c = v - mean
    inv = lax.rsqrt(jnp.mean(c * c, -1, keepdims=True) + 1e-12)
    return c * inv, inv


class Ring:
    def __init__(self, s, u, g, b, half, places, f, rd, where):
        self.s, self.u, self.g, self.b, self.half = s, u, g, b, half
        self.c_at, self.a_at, self.b_at, self.z_at = places
        self.f, self.rd = f, rd
        dp, psg = where
        self.z, self.x, self.y, self.c = dp // 2, lax.rem(dp, 2), psg // 2, lax.rem(psg, 2)
        self.core = {"psg": self.y * 2 + 1 - self.c}
        self.xn = {"dp": self.z * 2 + 1 - self.x}
        self.yn = {"psg": (1 - self.y) * 2 + self.c}
        self.zn = [{"dp": lax.rem(self.z + k, 4) * 2 + self.x} for k in range(1, 4)]

    def cols(self, c):
        return pl.ds(pl.multiple_of(c * self.half, 128), self.half)

    def part(self, row, n, c):
        return self.g.at[pl.ds(pl.multiple_of(row * self.b, 16), n * self.b), self.cols(c)]

    def remote(self, i, src, dst, dev):
        return pltpu.make_async_remote_copy(
            src_ref=src, dst_ref=dst, send_sem=self.s.gss.at[self.u, i], recv_sem=self.s.grs.at[self.u, i],
            device_id=dev, device_id_type=MESH,
        )

    def copy_c(self, z):
        return self.remote(z, self.part(4 * z, 4, 1 - self.c), self.c_at(z), self.core)

    def copy_a(self, z):
        if z % 2 == 0:
            return [self.remote(4 + z // 2, self.part(4 * z + 2 * (1 - self.x), 2, self.c), self.a_at(z, 0, 2), self.xn)]
        return [
            self.remote(
                6 + z - 1 + x, self.part(4 * z + 2 * x + 1 - self.y, 1, self.c), self.a_at(z, x, 1), self.yn
            )
            for x in range(2)
        ]

    def copy_b(self, z):
        if z % 2 == 0:
            return self.remote(10 + z, self.part(4 * z + 2 * self.x + 1 - self.y, 1, self.c), self.b_at(z), self.yn)
        return self.remote(10 + z, self.part(4 * z + 2 * (1 - self.x) + self.y, 1, self.c), self.b_at(z), self.xn)

    def copy_z(self, k):
        z = lax.rem(self.z + k + 1, 4)
        return self.remote(14 + k, self.part(4 * z + 2 * self.x + self.y, 1, self.c), self.z_at(k), self.zn[k])

    def copy_d(self):
        h = self.b // 2
        src = self.f.at[pl.ds(pl.multiple_of((1 - self.c) * h, 8), h), :]
        return self.remote(17, src, self.rd, self.core)

    def add(self, part, got):
        part[...] = part[...] + got[...]

    def step1(self):
        for z in range(4):
            self.copy_c(z).start()

    def step2(self):
        for z in range(4):
            self.copy_c(z).wait_recv()
            self.add(self.part(4 * z, 4, self.c), self.c_at(z))
            for c in self.copy_a(z):
                c.start()

    def step3(self):
        for z in range(4):
            for c in self.copy_a(z):
                c.wait_recv()
            if z % 2 == 0:
                self.add(self.part(4 * z + 2 * self.x, 2, self.c), self.a_at(z, 0, 2))
            else:
                for x in range(2):
                    self.add(self.part(4 * z + 2 * x + self.y, 1, self.c), self.a_at(z, x, 1))
            self.copy_b(z).start()

    def step4(self):
        for z in range(4):
            self.copy_b(z).wait_recv()
            self.add(self.part(4 * z + 2 * self.x + self.y, 1, self.c), self.b_at(z))
        for k in range(3):
            self.copy_z(k).start()

    def step5(self):
        v = self.part(4 * self.z + 2 * self.x + self.y, 1, self.c)[...].astype(F32)
        for k in range(3):
            self.copy_z(k).wait_recv()
            v = v + self.z_at(k)[...].astype(F32)
        self.f[...] = v
        self.copy_d().start()

    def step6(self, put):
        self.copy_d().wait_recv()
        h = self.b // 2
        put(self.c, self.f[pl.ds(pl.multiple_of(self.c * h, 8), h), :])
        put(1 - self.c, self.rd[...])

    def finish(self):
        for z in range(4):
            self.copy_c(z).wait_send()
            for c in self.copy_a(z):
                c.wait_send()
            self.copy_b(z).wait_send()
        for k in range(3):
            self.copy_z(k).wait_send()
        self.copy_d().wait_send()


def place(ref, f, n, width):
    def ref_at(i, x=0, m=1):
        row, col = f(i)
        return ref.at[row + x * n : row + x * n + m * n, col : col + width]

    return ref_at


def make_rings(s, cfg, where):
    D, FF = cfg.D, cfg.FF
    h, w, b, e = D // 2, FF // 2, D // 16, FF // 16
    low = D
    spots = lambda r, k: (
        place(r, lambda z: (low + 4 * b * (z % 2), (k + z // 2) * h), 4 * b, h),
        place(r, lambda z: (low + 2 * b * z, (k + 2) * h), b, h),
        place(r, lambda z: (low + b * z, (k + 3) * h), b, h),
        place(r, lambda z: (low + b * (4 + z), (k + 3) * h), b, h),
    )
    down = (
        place(s.hid, lambda z: (0, z * h), 4 * e, h),
        place(s.hid, lambda z: (2 * e * (z % 2), (4 + z // 2) * h), e, h),
        place(s.hid, lambda z: (e * z, 6 * h), e, h),
        place(s.hid, lambda z: (e * z, 7 * h), e, h),
    )
    up = (
        place(s.slo, lambda z: (4 * b * z, 0), 4 * b, w),
        place(s.slo, lambda z: (2 * b * z, w), b, w),
        place(s.slo, lambda z: (b * (8 + z), w), b, w),
        place(s.slo, lambda z: (b * (12 + z), w), b, w),
    )
    second = (
        place(s.y1, lambda z: (4 * b * z, 0), 4 * b, h),
        place(s.y1, lambda z: (low + 2 * b * z, 0), b, h),
        place(s.y1, lambda z: (b * z, h), b, h),
        place(s.y1, lambda z: (b * (4 + z), h), b, h),
    )
    third = (
        place(s.y1, lambda z: (b * (7 + 4 * z), h), 4 * b, h),
        place(s.hid, lambda z: (low + 2 * b * z, 4 * h), b, h),
        place(s.hid, lambda z: (low + b * z, 5 * h), b, h),
        place(s.hid, lambda z: (low + b * (4 + z), 5 * h), b, h),
    )
    small = (
        place(s.mrecv, lambda z: (4 * b * z, 0), 4 * b, 128),
        place(s.mrecv, lambda z: (b * (16 + 2 * z), 0), b, 128),
        place(s.mrecv, lambda z: (b * (24 + z), 0), b, 128),
        place(s.mrecv, lambda z: (b * (28 + z), 0), b, 128),
    )
    mk = lambda u, g, bb, half, places, f, rd: Ring(s, u, g, bb, half, places, f, rd, where)
    return (
        mk(0, s.wdn, e, h, down, s.fd, s.rd),
        mk(1, s.wup, b, w, up, s.fu, s.ru),
        mk(2, s.wout, b, h, spots(s.hid, 0), s.fq.at[0], s.rq.at[0]),
        mk(3, s.ctx, b, h, spots(s.slo, 0), s.fq.at[1], s.rq.at[1]),
        mk(4, s.fb, b, h, second, s.fq.at[2], s.rq.at[2]),
        mk(5, s.gb, b, h, third, s.fq.at[3], s.rq.at[3]),
        mk(6, s.misc, b, 128, small, s.fm, s.rm),
    )


def kernel(cfg, *refs):
    s = Space()
    for name, ref in zip(cfg.names, refs):
        setattr(s, name, ref)
    T, NP, NQ, TT = cfg.T, cfg.NP, cfg.NQ, cfg.TT
    D, FF = cfg.D, cfg.FF
    nrow = NP // LEN
    me_dp = lax.axis_index("dp")
    me_psg = lax.axis_index("psg")
    n_psg, n_dp = cfg.n_psg, cfg.n_dp

    def load(k, src, dst):
        c = pltpu.make_async_copy(src, dst, s.lsem.at[k])
        c.start()
        return c

    l_x = load(0, s.i_pass, s.x.at[0:NP])
    l_q = load(1, s.i_query, s.x.at[NP:T])
    l_wqkv = load(2, s.i_wqkv, s.wqkv)
    l_wout = load(3, s.i_wout, s.wout)
    l_wup = load(4, s.i_wup, s.wup)
    l_wdn = load(5, s.i_wdn, s.wdn)
    l_wpj = load(6, s.i_wproj, s.wproj)

    bar = pltpu.get_barrier_semaphore()
    peers = []
    for k in range(1, n_psg):
        peers.append({"psg": lax.rem(me_psg + k, n_psg)})
    if cfg.loss_here:
        for k in range(1, n_dp):
            peers.append({"dp": lax.rem(me_dp + k, n_dp)})
    for p in peers:
        pl.semaphore_signal(bar, inc=1, device_id=p, device_id_type=MESH)

    sums = cfg.sums
    if sums:
        ring_d, ring_u, ring_o, ring_1, ring_2, ring_3, ring_m = rings = make_rings(s, cfg, (me_dp, me_psg))

        def epoch_signal(k):
            for dev in [ring_d.core, ring_d.xn, ring_d.yn] + ring_d.zn:
                pl.semaphore_signal(s.epoch.at[k], inc=1, device_id=dev, device_id_type=MESH)

        def epoch_wait(k):
            pl.semaphore_wait(s.epoch.at[k], 6)

    def put_in(ref):
        def put(c, v):
            ref[:, pl.ds(pl.multiple_of(c * v.shape[1], 128), v.shape[1])] = v

        return put

    def put_group(g):
        def put(c, v):
            for i in range(v.shape[1] // 128):
                k = c * (v.shape[1] // 128) + i
                col = (k // 2) * D + g * 256 + lax.rem(k, 2) * 128
                s.o_qkv[:, pl.ds(pl.multiple_of(col, 128), 128)] = v[:, i * 128 : i * 128 + 128]

        return put

    lane = lax.broadcasted_iota(jnp.int32, (128, 128), 1)
    low_half = lane < 64
    zero_b = jnp.zeros((), BF)

    def halves(a):
        keep = lax.broadcasted_iota(jnp.int32, a.shape, 1) < 64
        return jnp.where(keep, a, zero_b), jnp.where(keep, zero_b, a)

    bounds = []
    for r in range(nrow):
        seg = s.i_seg[r : r + 1, :]
        bounds.append(
            (
                jnp.sum(jnp.where(seg < 1, 1.0, 0.0), axis=1, keepdims=True),
                jnp.sum(jnp.where(seg < 2, 1.0, 0.0), axis=1, keepdims=True),
            )
        )

    s.bqkv[...] = jnp.zeros_like(s.bqkv)
    s.bqkv[0:1, 0:D] = s.i_bq[...]
    s.bqkv[0:1, 2 * D : 3 * D] = s.i_bv[...]
    l_x.wait()
    l_q.wait()
    l_wqkv.wait()

    def qkv_body(n, _):
        c = at(n, 256)
        s.mixed[:, c] = (nn(s.x[...], s.wqkv[:, c]) + s.bqkv[0:1, c]).astype(BF)
        return 0

    lax.fori_loop(0, 3 * D // 256, qkv_body, 0)

    scale = 0.125 * LOG2E

    def p_copy_out(i, slot):
        return pltpu.make_async_copy(s.pbuf.at[slot], s.o_p.at[i], s.psem.at[slot])

    for r in range(nrow):
        b0, b1 = bounds[r]
        for qs, ks, kw, off in TILES:
            qi = (lax.broadcasted_iota(jnp.int32, (128, kw), 0) + qs).astype(F32)
            ki = (lax.broadcasted_iota(jnp.int32, (128, kw), 1) + ks).astype(F32)
            sq = jnp.where(qi >= b0, 1.0, 0.0) + jnp.where(qi >= b1, 1.0, 0.0)
            sk = jnp.where(ki >= b0, 1.0, 0.0) + jnp.where(ki >= b1, 1.0, 0.0)
            s.bias[:, off : off + kw] = jnp.where(sq == sk, 0.0, -1e30)

        def att_body(hp, _, r=r):
            i = r * (H // 2) + hp
            slot = lax.rem(i, 2)

            @pl.when(i >= 2)
            def _():
                p_copy_out(i - 2, slot).wait()

            cq, ck, cv = at(hp, 128), at(hp + D // 128, 128), at(hp + 2 * D // 128, 128)
            for qs, ks, kw, off in TILES:
                qh = halves(s.mixed[r * LEN + qs : r * LEN + qs + 128, cq])
                kt = s.mixed[r * LEN + ks : r * LEN + ks + kw, ck]
                vt = s.mixed[r * LEN + ks : r * LEN + ks + kw, cv]
                o = []
                for h in range(2):
                    sc = nt(qh[h], kt) * scale + s.bias[:, off : off + kw]
                    e = jnp.exp2(sc - jnp.max(sc, -1, keepdims=True))
                    p = (e * (1.0 / jnp.sum(e, -1, keepdims=True))).astype(BF)
                    s.pbuf[slot, h, :, off : off + kw] = p
                    o.append(nn(p, vt))
                s.ctx[r * LEN + qs : r * LEN + qs + 128, cq] = jnp.where(low_half, o[0], o[1]).astype(BF)
            p_copy_out(i, slot).start()
            return 0

        lax.fori_loop(0, H // 2, att_body, 0)

    qi = lax.broadcasted_iota(jnp.int32, (NQ, NQ), 0)
    ki = lax.broadcasted_iota(jnp.int32, (NQ, NQ), 1)
    ql = cfg.qlen
    qbias = jnp.where((qi // ql) == (ki // ql), 0.0, -1e30)
    for hp in range(H // 2):
        cq = slice(hp * 128, hp * 128 + 128)
        qh = halves(s.mixed[NP:T, hp * 128 : hp * 128 + 128])
        kt = s.mixed[NP:T, D + hp * 128 : D + hp * 128 + 128]
        vt = s.mixed[NP:T, 2 * D + hp * 128 : 2 * D + hp * 128 + 128]
        o = []
        for h in range(2):
            sc = nt(qh[h], kt) * scale + qbias
            e = jnp.exp2(sc - jnp.max(sc, -1, keepdims=True))
            p = (e * (1.0 / jnp.sum(e, -1, keepdims=True))).astype(BF)
            s.pq[hp, h] = p
            o.append(nn(p, vt))
        s.ctx[NP:T, cq] = jnp.where(low_half, o[0], o[1]).astype(BF)
    last = nrow * (H // 2)
    p_copy_out(last - 2, (last - 2) % 2).wait()
    p_copy_out(last - 1, (last - 1) % 2).wait()

    l_wout.wait()

    def out_body(t, _):
        rr = at(t, TT)
        v = nn(s.ctx[rr, :], s.wout[...]) + s.i_bout[...] + s.x[rr, :].astype(F32)
        y, inv = norm_stats(v)
        s.y1[rr, :] = y.astype(BF)
        s.st[rr, 0:1] = inv
        s.fb[rr, :] = (y * s.i_g1[...] + s.i_b1[...]).astype(BF)
        return 0

    lax.fori_loop(0, T // TT, out_body, 0)

    l_wup.wait()

    def up_body(n, _):
        c = at(n, 256)
        for m in range(T // TT):
            rr = slice(m * TT, m * TT + TT)
            h = nn(s.fb[rr, :], s.wup[:, c]) + s.i_bup[:, c]
            cdf = 0.5 * (1.0 + lax.erf(h * 0.7071067811865476))
            s.hid[rr, c] = (h * cdf).astype(BF)
            s.slo[rr, c] = (cdf + h * jnp.exp2(h * h * (-0.5 * LOG2E)) * 0.3989422804014327).astype(BF)
        return 0

    lax.fori_loop(0, FF // 256, up_body, 0)

    l_wdn.wait()
    l_wpj.wait()

    def down_body(t, _):
        rr = at(t, TT)
        first = s.y1[rr, :].astype(F32) * s.i_g1[...] + s.i_b1[...]
        v = first + (nn(s.hid[rr, :], s.wdn[...]) + s.i_bdn[...])
        y, inv = norm_stats(v)
        s.gs[rr, :] = y
        s.st[rr, 1:2] = inv
        sec = (y * s.i_g2[...] + s.i_b2[...]).astype(BF)
        s.gb[rr, :] = sec
        pj = nn(sec, s.wproj[...])
        il = lax.rsqrt(jnp.sum(pj * pj, -1, keepdims=True) + 1e-06)
        s.st[rr, 2:3] = il
        u = pj * il
        s.unit[rr, :] = u
        s.unitb[rr, :] = u.astype(BF)
        return 0

    lax.fori_loop(0, T // TT, down_body, 0)

    o_pe = pltpu.make_async_copy(s.unitb.at[0:NP], s.o_pe, s.osem.at[0])
    o_pe.start()
    o_qe = pltpu.make_async_copy(s.unitb.at[NP:T], s.o_qe, s.osem.at[1])
    o_qe.start()

    pl.semaphore_wait(bar, len(peers))
    sends = []

    def remote(src, dst, ssem, rsem, dev):
        c = pltpu.make_async_remote_copy(
            src_ref=src, dst_ref=dst, send_sem=ssem, recv_sem=rsem, device_id=dev, device_id_type=MESH
        )
        return c

    q_copies = []
    for k in range(1, n_psg):
        c = remote(
            s.unitb.at[NP:T], s.aq.at[k], s.ss.at[0, k], s.rs.at[0, k], {"psg": lax.rem(me_psg + k, n_psg)}
        )
        c.start()
        q_copies.append(c)
    s.aq[0] = s.unitb[NP:T, :]

    for r in range(nrow):
        b0, b1 = bounds[r]
        ti = lax.broadcasted_iota(jnp.int32, (LEN, 128), 0).astype(F32)
        li = lax.broadcasted_iota(jnp.int32, (LEN, 128), 1).astype(F32)
        pid = SEGS * r + jnp.where(ti >= b0, 1.0, 0.0) + jnp.where(ti >= b1, 1.0, 0.0)
        s.ind[r * LEN : (r + 1) * LEN, :] = jnp.where(pid == li, 1.0, 0.0).astype(BF)
    count = jnp.sum(s.ind[...].astype(F32), axis=0, keepdims=True)
    slots = nrow * SEGS
    valid = lax.broadcasted_iota(jnp.int32, (1, 128), 1) < slots
    count = jnp.where(valid, count, 1.0)
    nqg = NQ // ql
    s.lg[0] = jnp.zeros(s.lg.shape[1:], F32)

    def powers(k):
        sim = nt(s.aq[k], s.unitb[0:NP, :])
        return jnp.exp2((sim - 1.0) * (LOG2E / SHARP))

    for k in range(n_psg):
        if k:
            q_copies[k - 1].wait_recv()
        pw = powers(k)
        hi = pw.astype(BF)
        lo = (pw - hi.astype(F32)).astype(BF)
        tot = nn(hi, s.ind[...]) + nn(lo, s.ind[...])
        tot = jnp.where(valid, tot, 1.0)
        s.tot[k] = tot
        line = jnp.log(tot / count) + 1.0 / SHARP
        line = jnp.where(valid, line, 0.0)
        src = lax.rem(me_psg + n_psg - k, n_psg)
        s.line[rows_at(src * NQ, NQ, NQ), :] = line

    nq_all = n_psg * nqg
    qrow = lax.broadcasted_iota(jnp.int32, (nq_all, n_psg * NQ), 0) * ql
    qcol = lax.broadcasted_iota(jnp.int32, (nq_all, n_psg * NQ), 1)
    sel = jnp.where(jnp.logical_and(qcol >= qrow, qcol < qrow + ql), 1.0, 0.0).astype(BF)
    line = s.line[...]
    hi = line.astype(BF)
    line = line - hi.astype(F32)
    mid = line.astype(BF)
    lo = (line - mid.astype(F32)).astype(BF)
    s.lg[0, 0:nq_all, :] = nn(sel, hi) + (nn(sel, mid) + nn(sel, lo))
    s.lg[0, nq_all : 2 * nq_all, 0:slots] = s.i_teach[...]
    l_copies = []
    for k in range(1, n_psg):
        c = remote(
            s.lg.at[0], s.lg.at[k], s.ss.at[1, k], s.rs.at[1, k], {"psg": lax.rem(me_psg + k, n_psg)}
        )
        c.start()
        l_copies.append(c)
    for c in l_copies:
        c.wait_recv()
    ok = valid[None]
    lg = s.lg[...]
    half = nq_all

    def log_norm(v):
        vm = jnp.where(valid[None], v, -1e30)
        top = jnp.max(jnp.max(vm, axis=-1, keepdims=True), axis=0, keepdims=True)
        sh = v - top
        ex = jnp.where(valid[None], jnp.exp(sh), 0.0)
        tot = jnp.sum(jnp.sum(ex, axis=-1, keepdims=True), axis=0, keepdims=True)
        return sh - jnp.log(tot)

    stu = log_norm(lg[:, 0:half, :])
    tea = log_norm(lg[:, half : 2 * half, :])
    pt = jnp.exp(tea)
    kl = jnp.where(ok, pt * (tea - stu), 0.0)
    group_sum = jnp.sum(jnp.sum(jnp.sum(kl, axis=0), axis=-1, keepdims=True), axis=0, keepdims=True)
    s.ls[0] = jnp.broadcast_to(group_sum / n_dp, (8, 128))
    loss_copies = []
    if cfg.loss_here:
        for k in range(1, n_dp):
            c = remote(
                s.ls.at[0], s.ls.at[k], s.lss.at[k], s.lrs.at[k], {"dp": lax.rem(me_dp + k, n_dp)}
            )
            c.start()
            loss_copies.append(c)
    s.gl[...] = jnp.where(valid, (jnp.exp(stu[0]) - pt[0]) / n_dp, 0.0)
    for q in range(nq_all):
        s.line[q * ql : q * ql + ql, :] = jnp.broadcast_to(s.gl[q : q + 1, :], (ql, 128))

    g_copies = []
    for k in list(range(1, n_psg)) + [0]:
        pw = powers(k)
        src = lax.rem(me_psg + n_psg - k, n_psg)
        ratio = s.line[rows_at(src * NQ, NQ, NQ), :] / s.tot[k]
        ratio = ratio * (1.0 / SHARP)
        hi = ratio.astype(BF)
        lo = (ratio - hi.astype(F32)).astype(BF)
        g = ((nt(hi, s.ind[...]) + nt(lo, s.ind[...])) * pw).astype(BF)
        s.gsim[k * NQ : (k + 1) * NQ, :] = g
        qp = nn(g, s.unitb[0:NP, :])
        if k:
            s.qs[k] = qp.astype(BF)
            c = remote(s.qs.at[k], s.qr.at[k], s.ss.at[2, k], s.rs.at[2, k], {"psg": src})
            c.start()
            g_copies.append(c)
        else:
            s.own[...] = qp

    def unit_back(gu, rr):
        u = s.unit[rr, :]
        return (s.st[rr, 2:3] * (gu - u * jnp.sum(gu * u, -1, keepdims=True))).astype(BF)

    aq = s.aq[...].reshape(n_psg * NQ, 128)
    for m in range(NP // 256):
        rr = slice(m * 256, m * 256 + 256)
        gu = tn(s.gsim[:, rr], aq)
        s.gp[rr, :] = unit_back(gu, rr)
    for c in g_copies:
        c.wait_recv()
    gu = s.own[...]
    for k in range(1, n_psg):
        gu = gu + s.qr[k].astype(F32)
    s.gp[NP:T, :] = unit_back(gu, slice(NP, T))

    s.misc[:, 0:128] = tn(s.gb[...], s.gp[...]).astype(BF)

    s.vr[...] = jnp.zeros_like(s.vr)

    def addrow(k, v):
        s.vr[k : k + 1, :] = s.vr[k : k + 1, :] + jnp.sum(v, axis=0, keepdims=True)

    def norm2_body(t, _):
        rr = at(t, TT)
        g = nt(s.gp[rr, :], s.wproj[...])
        y = s.gs[rr, :]
        addrow(6, g * y)
        addrow(7, g)
        d = g * s.i_g2[...]
        gs = s.st[rr, 1:2] * (d - jnp.mean(d, -1, keepdims=True) - y * jnp.mean(d * y, -1, keepdims=True))
        s.gs[rr, :] = gs
        b = gs.astype(BF)
        s.gb[rr, :] = b
        addrow(5, b.astype(F32))
        return 0

    lax.fori_loop(0, T // TT, norm2_body, 0)

    def ff_body(n, _):
        c = at(n, 256)
        w = s.wdn[c, :]
        tot = jnp.zeros((1, 256), F32)
        for m in range(T // TT):
            rr = slice(m * TT, m * TT + TT)
            g = (nt(s.gb[rr, :], w) * s.slo[rr, c].astype(F32)).astype(BF)
            s.slo[rr, c] = g
            tot = tot + jnp.sum(g.astype(F32), axis=0, keepdims=True)
        s.bup[0:1, c] = tot
        s.wdn[c, :] = tn(s.hid[:, c], s.gb[...]).astype(BF)
        return 0

    lax.fori_loop(0, FF // 256, ff_body, 0)

    if sums:
        epoch_signal(0)

    def norm1_body(t, _):
        rr = at(t, TT)
        g = s.gs[rr, :] + nt(s.slo[rr, :], s.wup[...])
        y = s.y1[rr, :].astype(F32)
        addrow(3, g * y)
        addrow(4, g)
        d = g * s.i_g1[...]
        gs = s.st[rr, 0:1] * (d - jnp.mean(d, -1, keepdims=True) - y * jnp.mean(d * y, -1, keepdims=True))
        s.gs[rr, :] = gs
        b = gs.astype(BF)
        s.gb[rr, :] = b
        addrow(2, b.astype(F32))
        return 0

    lax.fori_loop(0, T // TT, norm1_body, 0)

    def gup_body(n, _):
        c = at(n, 256)
        s.wup[:, c] = tn(s.fb[...], s.slo[:, c]).astype(BF)
        return 0

    if sums:
        epoch_wait(0)
        ring_d.step1()
    lax.fori_loop(0, FF // 512, gup_body, 0)
    if sums:
        ring_d.step2()
    lax.fori_loop(FF // 512, FF // 256, gup_body, 0)
    if sums:
        epoch_signal(1)
        ring_d.step3()

    def dctx_body(t, _):
        rr = at(t, TT)
        s.dctx[rr, :] = nt(s.gb[rr, :], s.wout[...]).astype(BF)
        return 0

    lax.fori_loop(0, T // TT, dctx_body, 0)
    if sums:
        ring_d.step4()
        epoch_wait(1)
        ring_u.step1()
    s.wout[...] = tn(s.ctx[...], s.gb[...]).astype(BF)
    if sums:
        ring_o.step1()
        ring_d.step5()

    def p_copy_in(j):
        g, rest = j // (2 * nrow), lax.rem(j, 2 * nrow)
        i = (rest // 2) * (H // 2) + 2 * g + lax.rem(rest, 2)
        slot = lax.rem(j, 2)
        return pltpu.make_async_copy(s.o_p.at[i], s.pbuf.at[slot], s.psem.at[slot])

    steps = nrow * (H // 2)
    p_copy_in(0).start()

    def att_back(j, _):
        g, rest = j // (2 * nrow), lax.rem(j, 2 * nrow)
        r = rest // 2
        hp = 2 * g + lax.rem(rest, 2)
        slot = lax.rem(j, 2)

        @pl.when(j + 1 < steps)
        def _():
            p_copy_in(j + 1).start()

        p_copy_in(j).wait()
        cq, ck, cv = at(hp, 128), at(hp + D // 128, 128), at(hp + 2 * D // 128, 128)
        base = r * LEN

        def rws(a, n):
            return pl.ds(pl.multiple_of(base + a, 128), n)

        for qs, ks, kw, off in TILES:
            do = halves(s.dctx[rws(qs, 128), cq])
            kt = s.mixed[rws(ks, kw), ck]
            vt = s.mixed[rws(ks, kw), cv]
            dq = []
            for h in range(2):
                p = s.pbuf[slot, h, :, off : off + kw].astype(F32)
                dp = nt(do[h], vt)
                pd = p * dp
                ds = (pd - p * jnp.sum(pd, -1, keepdims=True)).astype(BF)
                s.ds[h, :, off : off + kw] = ds
                dq.append(nn(ds, kt))
            s.dq[qs : qs + 128, :] = (jnp.where(low_half, dq[0], dq[1]) * 0.125).astype(BF)
        for kk in range(4):
            dk = [None, None]
            dv = [None, None]
            for h in range(2):
                for qs, ks, kw, off in TILES:
                    rel = kk * 128 - ks
                    if rel < 0 or rel >= kw:
                        continue
                    qt = s.mixed[rws(qs, 128), cq]
                    ot = s.dctx[rws(qs, 128), cq]
                    a = tn(s.ds[h, :, off + rel : off + rel + 128], qt)
                    b = tn(s.pbuf[slot, h, :, off + rel : off + rel + 128], ot)
                    dk[h] = a if dk[h] is None else dk[h] + a
                    dv[h] = b if dv[h] is None else dv[h] + b
            s.dk[kk * 128 : kk * 128 + 128, :] = (jnp.where(low_half, dk[0], dk[1]) * 0.125).astype(BF)
            s.dv[kk * 128 : kk * 128 + 128, :] = jnp.where(low_half, dv[0], dv[1]).astype(BF)
        s.mixed[rws(0, LEN), cq] = s.dq[...]
        s.mixed[rws(0, LEN), ck] = s.dk[...]
        s.mixed[rws(0, LEN), cv] = s.dv[...]
        return 0

    def att_back_q(hp, _):
        cq, ck, cv = at(hp, 128), at(hp + D // 128, 128), at(hp + 2 * D // 128, 128)
        qt = s.mixed[NP:T, cq]
        kt = s.mixed[NP:T, ck]
        vt = s.mixed[NP:T, cv]
        ot = s.dctx[NP:T, cq]
        do = halves(ot)
        dq, dk, dv = [], [], []
        for h in range(2):
            pb = s.pq[hp, h]
            p = pb.astype(F32)
            pd = p * nt(do[h], vt)
            ds = (pd - p * jnp.sum(pd, -1, keepdims=True)).astype(BF)
            dq.append(nn(ds, kt))
            dk.append(tn(ds, qt))
            dv.append(tn(pb, ot))
        s.mixed[NP:T, cq] = (jnp.where(low_half, dq[0], dq[1]) * 0.125).astype(BF)
        s.mixed[NP:T, ck] = (jnp.where(low_half, dk[0], dk[1]) * 0.125).astype(BF)
        s.mixed[NP:T, cv] = jnp.where(low_half, dv[0], dv[1]).astype(BF)
        return 0

    lax.fori_loop(0, H // 2, att_back_q, 0)

    groups = (s.ctx, s.fb, s.gb)

    def group_grad(g):
        for w in range(3):
            c = w * D + g * 256
            groups[g][0:D, w * 256 : w * 256 + 256] = tn(s.x[...], s.mixed[:, c : c + 256]).astype(BF)

    def step(j, _):
        att_back(j, 0)
        if sums:

            @pl.when(j == 1)
            def _():
                ring_u.step2()
                ring_o.step2()

            @pl.when(j == 2)
            def _():
                ring_d.step6(put_in(s.o_dn))

        @pl.when(j == 3)
        def _():
            group_grad(0)
            if sums:
                ring_1.step1()

        if sums:

            @pl.when(j == 5)
            def _():
                ring_u.step3()
                ring_o.step3()
                ring_1.step2()

        @pl.when(j == 7)
        def _():
            group_grad(1)
            if sums:
                ring_2.step1()
                ring_u.step4()
                ring_o.step4()
                ring_1.step3()

        if sums:

            @pl.when(j == 9)
            def _():
                ring_u.step5()
                ring_o.step5()
                ring_1.step4()
                ring_2.step2()

        return 0

    lax.fori_loop(0, steps, step, 0)
    group_grad(2)
    if sums:
        ring_3.step1()
    for w, k in ((0, 0), (2, 1)):
        s.vr[k : k + 1, :] = jnp.sum(s.mixed[:, w * D : w * D + D].astype(F32), axis=0, keepdims=True)

    if sums:
        pad = jnp.zeros((120, 128), F32)
        for i in range(D // 128):
            v = s.vr[:, i * 128 : i * 128 + 128]
            s.vcol[i * 128 : i * 128 + 128, :] = jnp.concatenate([v, pad], 0).T
        q = D // 32
        lane = lax.broadcasted_iota(jnp.int32, (q, 128), 1)
        for i in range(FF // 384):
            for k in range(3):
                v = s.bup[0:1, i * 384 + k * 128 : i * 384 + k * 128 + 128]
                s.tcol[k * 128 : k * 128 + 128, :] = jnp.broadcast_to(v, (128, 128)).T
            for d in range(4):
                rr = slice((4 * i + d) * q, (4 * i + d) * q + q)
                v = s.vcol[rr, :]
                for k in range(4):
                    v = jnp.where(lane == 8 + k, s.tcol[(4 * d + k) * q : (4 * d + k) * q + q, :], v)
                s.vcol[rr, :] = v
        s.misc[:, 128:256] = s.vcol[...].astype(BF)
        ring_m.step1()
        ring_u.step6(put_in(s.o_up))
        ring_o.step6(put_in(s.o_out))
        ring_1.step5()
        ring_2.step3()

    def dx_body(t, _):
        rr = at(t, TT)
        s.gs[rr, :] = s.gs[rr, :] + nt(s.mixed[rr, :], s.wqkv[...])
        return 0

    lax.fori_loop(0, T // TT // 2, dx_body, 0)
    if sums:
        ring_3.step2()
        ring_m.step2()
        ring_2.step4()
        ring_1.step6(put_group(0))
    lax.fori_loop(T // TT // 2, T // TT, dx_body, 0)
    outs = [
        pltpu.make_async_copy(s.gs.at[0:NP], s.o_gp, s.osem.at[2]),
        pltpu.make_async_copy(s.gs.at[NP:T], s.o_gq, s.osem.at[3]),
    ]
    if not sums:
        outs += [
            pltpu.make_async_copy(s.wdn, s.o_dn, s.osem.at[4]),
            pltpu.make_async_copy(s.wup, s.o_up, s.osem.at[5]),
            pltpu.make_async_copy(s.wout, s.o_out, s.osem.at[6]),
            pltpu.make_async_copy(s.ctx.at[0:D], s.o_q.at[0], s.osem.at[7]),
            pltpu.make_async_copy(s.fb.at[0:D], s.o_q.at[1], s.osem.at[8]),
            pltpu.make_async_copy(s.gb.at[0:D], s.o_q.at[2], s.osem.at[9]),
            pltpu.make_async_copy(s.misc, s.o_misc, s.osem.at[10]),
        ]
        s.o_bup[...] = s.bup[0:1, :]
        s.o_vr[...] = s.vr[...]
    for c in outs:
        c.start()
    if sums:
        ring_3.step3()
        ring_m.step3()
        ring_2.step5()
        ring_3.step4()
        ring_m.step4()
        ring_2.step6(put_group(1))
        ring_3.step5()
        ring_m.step5()
        ring_3.step6(put_group(2))
        ring_m.step6(put_in(s.o_misc))
        for r in rings:
            r.finish()
    for c in q_copies + l_copies + g_copies + loss_copies:
        c.wait_send()
    for c in loss_copies:
        c.wait_recv()
    if cfg.loss_here:
        s.o_loss[...] = jnp.sum(s.ls[...], axis=0)
    else:
        s.o_loss[...] = s.ls[0]
    for c in [o_pe, o_qe] + outs:
        c.wait()


def make_body(n_dp, n_psg):
    def body(
        passage_states, segment_ids, query_states, teacher_scores,
        w_qkv, bias_q, bias_v, w_out, bias_out, ln1_gain, ln1_bias,
        w_up, bias_up, w_down, bias_down, ln2_gain, ln2_bias, w_proj,
    ):
        D, FF = w_up.shape
        E = w_proj.shape[1]
        rows, length, _ = passage_states.shape
        qn, ql, _ = query_states.shape
        NP, NQ = rows * length, qn * ql
        T = NP + NQ
        cfg = Space()
        cfg.T, cfg.NP, cfg.NQ, cfg.TT = T, NP, NQ, T // 4
        cfg.D, cfg.FF, cfg.qlen = D, FF, ql
        cfg.n_dp, cfg.n_psg = n_dp, n_psg
        cfg.loss_here = n_dp <= 16
        cfg.sums = n_dp == 8 and n_psg == 4
        npair = rows * (H // 2)
        any_spec = pl.BlockSpec(memory_space=pl.ANY)
        vm = pl.BlockSpec(memory_space=pltpu.VMEM)
        row = lambda v: v.reshape(1, -1)
        ins = [
            ("i_pass", passage_states.reshape(NP, D), any_spec),
            ("i_query", query_states.reshape(NQ, D), any_spec),
            ("i_seg", segment_ids, vm),
            ("i_teach", teacher_scores, vm),
            ("i_wqkv", w_qkv, any_spec),
            ("i_bq", row(bias_q), vm),
            ("i_bv", row(bias_v), vm),
            ("i_wout", w_out, any_spec),
            ("i_bout", row(bias_out), vm),
            ("i_g1", row(ln1_gain), vm),
            ("i_b1", row(ln1_bias), vm),
            ("i_wup", w_up, any_spec),
            ("i_bup", row(bias_up), vm),
            ("i_wdn", w_down, any_spec),
            ("i_bdn", row(bias_down), vm),
            ("i_g2", row(ln2_gain), vm),
            ("i_b2", row(ln2_bias), vm),
            ("i_wproj", w_proj, any_spec),
        ]
        sd = jax.ShapeDtypeStruct
        outs = [
            ("o_pe", sd((NP, E), BF), any_spec),
            ("o_qe", sd((NQ, E), BF), any_spec),
            ("o_loss", sd((8, 128), F32), vm),
            ("o_gp", sd((NP, D), F32), any_spec),
            ("o_gq", sd((NQ, D), F32), any_spec),
            ("o_p", sd((npair, 2, 128, PW), BF), any_spec),
        ]
        n_dev = n_dp * n_psg
        if cfg.sums:
            outs += [
                ("o_dn", sd((FF // n_dev, D), F32), vm),
                ("o_up", sd((D // n_dev, FF), F32), vm),
                ("o_out", sd((D // n_dev, D), F32), vm),
                ("o_qkv", sd((D // n_dev, 3 * D), F32), vm),
                ("o_misc", sd((D // n_dev, 256), F32), vm),
            ]
        else:
            outs += [
                ("o_dn", sd((FF, D), BF), any_spec),
                ("o_up", sd((D, FF), BF), any_spec),
                ("o_out", sd((D, D), BF), any_spec),
                ("o_q", sd((3, D, D), BF), any_spec),
                ("o_misc", sd((D, 256), BF), any_spec),
                ("o_bup", sd((1, FF), F32), vm),
                ("o_vr", sd((8, D), F32), vm),
            ]
        V = pltpu.VMEM
        DMA = pltpu.SemaphoreType.DMA
        scratch = [
            ("x", V((T, D), BF)),
            ("wqkv", V((D, 3 * D), BF)),
            ("wout", V((D, D), BF)),
            ("wup", V((D, FF), BF)),
            ("wdn", V((FF, D), BF)),
            ("wproj", V((D, E), BF)),
            ("bqkv", V((8, 3 * D), F32)),
            ("mixed", V((T, 3 * D), BF)),
            ("pbuf", V((2, 2, 128, PW), BF)),
            ("pq", V((H // 2, 2, NQ, NQ), BF)),
            ("bias", V((128, PW), F32)),
            ("ctx", V((T, D), BF)),
            ("y1", V((T, D), BF)),
            ("fb", V((T, D), BF)),
            ("hid", V((T, FF), BF)),
            ("slo", V((T, FF), BF)),
            ("gs", V((T, D), F32)),
            ("gb", V((T, D), BF)),
            ("st", V((T, 128), F32)),
            ("unit", V((T, E), F32)),
            ("unitb", V((T, E), BF)),
            ("aq", V((n_psg, NQ, E), BF)),
            ("ind", V((NP, 128), BF)),
            ("tot", V((n_psg, NQ, 128), F32)),
            ("lg", V((n_psg, 2 * n_psg * qn, 128), F32)),
            ("line", V((n_psg * NQ, 128), F32)),
            ("gl", V((n_psg * qn, 128), F32)),
            ("ls", V((n_dp if cfg.loss_here else 1, 8, 128), F32)),
            ("gsim", V((n_psg * NQ, NP), BF)),
            ("qs", V((n_psg, NQ, E), BF)),
            ("qr", V((n_psg, NQ, E), BF)),
            ("own", V((NQ, E), F32)),
            ("gp", V((T, E), BF)),
            ("misc", V((D, 256), BF)),
            ("vr", V((8, D), F32)),
            ("vcol", V((D, 128), F32)),
            ("bup", V((8, FF), F32)),
            ("dctx", V((T, D), BF)),
            ("ds", V((2, 128, PW), BF)),
            ("dq", V((LEN, 128), BF)),
            ("dk", V((LEN, 128), BF)),
            ("dv", V((LEN, 128), BF)),
            ("lsem", DMA((7,))),
            ("psem", DMA((2,))),
            ("osem", DMA((11,))),
            ("ss", DMA((3, n_psg))),
            ("rs", DMA((3, n_psg))),
            ("lss", DMA((n_dp,))),
            ("lrs", DMA((n_dp,))),
        ]
        if cfg.sums:
            b, e = D // 16, FF // 16
            scratch += [
                ("tcol", V((384, 128), F32)),
                ("mrecv", V((31 * b, 128), BF)),
                ("fd", V((e, D // 2), F32)),
                ("rd", V((e // 2, D // 2), F32)),
                ("fu", V((b, FF // 2), F32)),
                ("ru", V((b // 2, FF // 2), F32)),
                ("fq", V((4, b, D // 2), F32)),
                ("rq", V((4, b // 2, D // 2), F32)),
                ("fm", V((b, 128), F32)),
                ("rm", V((b // 2, 128), F32)),
                ("gss", DMA((7, 18))),
                ("grs", DMA((7, 18))),
                ("epoch", pltpu.SemaphoreType.REGULAR((2,))),
            ]
        cfg.names = [a for a, *_ in ins] + [a for a, *_ in outs] + [a for a, _ in scratch]
        res = pl.pallas_call(
            functools.partial(kernel, cfg),
            out_shape=[o[1] for o in outs],
            in_specs=[i[2] for i in ins],
            out_specs=[o[2] for o in outs],
            scratch_shapes=[v for _, v in scratch],
            compiler_params=pltpu.CompilerParams(
                collective_id=0, has_side_effects=True, vmem_limit_bytes=64 * 1024 * 1024 - 65536
            ),
        )(*[i[1] for i in ins])
        o = dict(zip([a for a, *_ in outs], res))
        loss = o["o_loss"][0, 0]
        if not cfg.loss_here:
            loss = lax.psum(loss, "dp")
        head = (
            o["o_pe"].reshape(rows, length, E),
            o["o_qe"].reshape(qn, ql, E),
            loss,
            o["o_gp"].reshape(rows, length, D),
            o["o_gq"].reshape(qn, ql, D),
        )
        if cfg.sums:
            m = o["o_misc"]
            vec = [m[:, 128 + k] for k in range(8)]
            g_bup = m[:, 136:140].T.reshape(-1)
            g_qkv, g_out, g_up, g_dn, g_proj = o["o_qkv"], o["o_out"], o["o_up"], o["o_dn"], m[:, 0:128]
        else:
            q3 = o["o_q"].reshape(3, D, 3, 256)
            q3 = jnp.transpose(q3, (1, 2, 0, 3)).reshape(D, 3 * D)

            def scat(v):
                return lax.psum_scatter(v, ("dp", "psg"), scatter_dimension=0, tiled=True)

            vec = scat(o["o_vr"].T)
            vec = [vec[:, k] for k in range(8)]
            g_bup = scat(o["o_bup"].reshape(-1))
            g_qkv, g_out, g_up, g_dn, g_proj = [
                scat(v.astype(F32)) for v in (q3, o["o_out"], o["o_up"], o["o_dn"], o["o_misc"][:, 0:128])
            ]
        return head + (
            g_qkv, vec[0], vec[1], g_out, vec[2], vec[3], vec[4],
            g_up, g_bup, g_dn, vec[5], vec[6], vec[7], g_proj,
        )

    return body


def solution(mesh):
    rowspec = P(("dp", "psg"))
    three = P(("dp", "psg"), None, None)
    two = P(("dp", "psg"), None)
    in_specs = (three, two, three, P("dp", "psg")) + (P(),) * 14
    out_specs = (
        three, three, P(), three, three,
        two, rowspec, rowspec, two, rowspec, rowspec, rowspec,
        two, rowspec, two, rowspec, rowspec, rowspec, two,
    )
    body = make_body(mesh.shape["dp"], mesh.shape["psg"])
    return jax.shard_map(body, mesh=mesh, in_specs=in_specs, out_specs=out_specs, check_vma=False)
```

time: 923 us -> 257 us (0.28)
  waiting for transfers between devices: 442 us -> 0 us
  matrix products: 242 us -> 0 us
  Pallas kernels: 0 us -> 227 us
  blocking collectives: 79.4 us -> 0 us
  other arithmetic: 69.2 us -> 0 us
  local copies, waits for them, and re-layouts: 64 us -> 27.9 us
  between operations: 16.7 us -> 0.69 us
    reduce_scatter x4 -> x0, waiting for transfers between devices: 317 us -> none  [the longest x1 142 us: body(): lax.psum_scatter(g_down, ('dp', 'psg'), scatter_dimension=0, tiled=True)]
    dot_general x47 -> x0, matrix products: 242 us -> none  [the longest x2 23.5 us: encode_back(): jnp.einsum('bqhe,bkhe->bhqk', grad_context, content_headwise, preferred_e...]
    pallas_call x0 -> x1, Pallas kernels: none -> 227 us  [body(): pl.pallas_call(functools.partial(kernel, cfg), out_shape=[o[1] for o in o...]
    unnamed x8 -> x0, waiting for transfers between devices: 125 us -> none
    unnamed x1 -> x0, blocking collectives: 41.3 us -> none
    reduce_sum x18 -> x0, other arithmetic: 31.8 us -> none  [the longest x2 11.3 us: encode(): total = jnp.sum(power_entries, -1, keepdims=True)]
    convert_element_type x6 -> x0, other arithmetic: 24.2 us -> none  [the longest x2 22.9 us: encode_back(): (probs * (grad_probs - jnp.sum(probs * grad_probs, -1, keepdims=True))).a...]
    all_gather x3 -> x0, blocking collectives: 19.7 us -> none  [the longest x1 7.88 us: body(): lax.all_gather(teacher_scores, 'psg', axis=1, tiled=True)]
  transfers between devices with their start and end apart: 6 -> 0, of which waited for: 4 -> 0; matrix products, arithmetic and copies ran while one was open for 27% -> 0% of each run, Pallas kernels for 0% -> 0%
where the time goes in v1:
time: 257 us; the launch traced here: 256 us
  Pallas kernels  227 us (88%)
  local copies, waits for them, and re-layouts  27.9 us (11%)
    pallas_call x1, Pallas kernels, body(): pl.pallas_call(functools.partial(kernel, cfg), out_shape=[o[1] for o in o...  227 us
    unnamed x19, local copies, waits for them, and re-layouts  11.7 us
    reshape x8, local copies, waits for them, and re-layouts, body(): row = lambda v: v.reshape(1, -1)  10.1 us

profile of v1, /device:TPU:1, one launch (start us, length us, event | category | flops | bytes accessed | tf_op | source)
XLA Modules:
  0.0 256.0 jit_solution(2000781248362030798)
XLA Ops:
  0.7 1.3 reshape.88.refs_5_
  1.9 1.3 reshape.89.refs_6_
  3.2 1.3 reshape.90.refs_8_
  4.5 1.3 reshape.91.refs_9_
  5.7 1.3 reshape.92.refs_10_
  7.0 1.3 reshape.94.refs_14_
  8.3 1.3 reshape.95.refs_15_
  9.5 1.3 reshape.96.refs_16_
  10.8 1.4 copy.39.refs_3_
  12.2 227.3 %shard_map.321 = (bf16[1024,128]{1,0:T(8,128)(2,1)}, bf16[128,128]{1,0:T(8,128)(2,1)}, f32[8,128]{1,0:T(8,128)}, f32[1024,768]{1,0:T(8,128)}, f32[128,768]{1,0:T...) custom-call(bf16[1024,768]{1,0:T(8,128)(2,1)} %bitcast.11, ...), custom_call_target="tpu_custom_call" | custom-call | tf_op jit(solution)/shard_map/pallas_call | solution.py:1015
  239.5 0.0 copy-start
  239.5 1.2 slice.33
  240.8 2.1 slice_reduce_fusion
  242.8 0.8 slice_bitcast_fusion
  243.6 1.3 slice.43
  244.9 0.1 copy.40
  245.0 0.6 reshape.101
  245.6 1.7 copy.49
  247.3 1.4 copy.50
  248.6 0.0 copy-start.3
  248.6 0.0 copy-start.4
  248.6 3.8 %copy.51 = f32[2,512,768]{2,1,0:T(8,128)} copy(f32[2,512,768]{2,1,0:T(8,128)} %bitcast.10) | data formatting | bytes 6291456
  252.5 0.0 copy-done
  252.5 0.7 copy.52
  253.2 0.0 copy-done.3
  253.2 0.7 copy.53
  253.9 0.0 copy-done.4
  253.9 0.6 copy.54
  254.6 0.0 copy-done.2
  254.6 0.7 copy.55
  255.3 0.0 copy-done.1
  255.3 0.7 copy.56
  (2 shorter events, 0.0 us)
Async XLA Ops:
  239.5 13.0 %copy-start = (f32[128,768]{1,0:T(8,128)S(1)}, f32[128,768]{1,0:T(8,128)}, u32[]{:S(2)}) copy-start(f32[128,768]{1,0:T(8,128)} %get-tuple-element.33) | copy-start | bytes 1179652
  248.6 4.6 %copy-start.3 = (f32[24,2304]{1,0:T(8,128)S(1)}, f32[24,2304]{1,0:T(8,128)}, u32[]{:S(2)}) copy-start(f32[24,2304]{1,0:T(8,128)} %get-tuple-element.71) | copy-start | bytes 663556
  248.6 5.3 %copy-start.4 = (f32[24,768]{1,0:T(8,128)S(1)}, f32[24,768]{1,0:T(8,128)}, u32[]{:S(2)}) copy-start(f32[24,768]{1,0:T(8,128)} %get-tuple-element.74) | copy-start | bytes 221188
  248.6 5.9 %copy-start.2 = (f32[24,3072]{1,0:T(8,128)S(1)}, f32[24,3072]{1,0:T(8,128)}, u32[]{:S(2)}) copy-start(f32[24,3072]{1,0:T(8,128)} %get-tuple-element.78) | copy-start | bytes 884740
  248.6 6.6 %copy-start.1 = (f32[96,768]{1,0:T(8,128)S(1)}, f32[96,768]{1,0:T(8,128)}, u32[]{:S(2)}) copy-start(f32[96,768]{1,0:T(8,128)} %get-tuple-element.80) | copy-start | bytes 884740

commit v2 on v1

--- a/solution.py
+++ b/solution.py
@@ -105,19 +105,19 @@
     def add(self, part, got):
         part[...] = part[...] + got[...]
 
-    def step1(self):
-        for z in range(4):
+    def start(self, *zs):
+        for z in zs:
             self.copy_c(z).start()
 
-    def step2(self):
-        for z in range(4):
+    def to_a(self, *zs):
+        for z in zs:
             self.copy_c(z).wait_recv()
             self.add(self.part(4 * z, 4, self.c), self.c_at(z))
             for c in self.copy_a(z):
                 c.start()
 
-    def step3(self):
-        for z in range(4):
+    def to_b(self, *zs):
+        for z in zs:
             for c in self.copy_a(z):
                 c.wait_recv()
             if z % 2 == 0:
@@ -127,14 +127,15 @@
                     self.add(self.part(4 * z + 2 * x + self.y, 1, self.c), self.a_at(z, x, 1))
             self.copy_b(z).start()
 
-    def step4(self):
-        for z in range(4):
+    def to_z(self, *zs):
+        for z in zs:
             self.copy_b(z).wait_recv()
             self.add(self.part(4 * z + 2 * self.x + self.y, 1, self.c), self.b_at(z))
-        for k in range(3):
-            self.copy_z(k).start()
-
-    def step5(self):
+        if zs[-1] == 3:
+            for k in range(3):
+                self.copy_z(k).start()
+
+    def to_core(self):
         v = self.part(4 * self.z + 2 * self.x + self.y, 1, self.c)[...].astype(F32)
         for k in range(3):
             self.copy_z(k).wait_recv()
@@ -142,7 +143,7 @@
         self.f[...] = v
         self.copy_d().start()
 
-    def step6(self, put):
+    def out(self, put):
         self.copy_d().wait_recv()
         h = self.b // 2
         put(self.c, self.f[pl.ds(pl.multiple_of(self.c * h, 8), h), :])
@@ -212,9 +213,9 @@
         mk(0, s.wdn, e, h, down, s.fd, s.rd),
         mk(1, s.wup, b, w, up, s.fu, s.ru),
         mk(2, s.wout, b, h, spots(s.hid, 0), s.fq.at[0], s.rq.at[0]),
-        mk(3, s.ctx, b, h, spots(s.slo, 0), s.fq.at[1], s.rq.at[1]),
-        mk(4, s.fb, b, h, second, s.fq.at[2], s.rq.at[2]),
-        mk(5, s.gb, b, h, third, s.fq.at[3], s.rq.at[3]),
+        mk(3, s.fb, b, h, spots(s.slo, 0), s.fq.at[1], s.rq.at[1]),
+        mk(4, s.gb, b, h, second, s.fq.at[2], s.rq.at[2]),
+        mk(5, s.ctx, b, h, third, s.fq.at[3], s.rq.at[3]),
         mk(6, s.misc, b, 128, small, s.fm, s.rm),
     )
 
@@ -243,6 +244,9 @@
     l_wdn = load(5, s.i_wdn, s.wdn)
     l_wpj = load(6, s.i_wproj, s.wproj)
 
+    for k, v in enumerate((s.i_bout, s.i_g1, s.i_b1, s.i_bdn, s.i_g2, s.i_b2)):
+        s.vin[k : k + 1, :] = v[...][None, :]
+    v_bout, v_g1, v_b1, v_bdn, v_g2, v_b2 = [s.vin.at[k : k + 1] for k in range(6)]
     bar = pltpu.get_barrier_semaphore()
     peers = []
     for k in range(1, n_psg):
@@ -261,8 +265,33 @@
             for dev in [ring_d.core, ring_d.xn, ring_d.yn] + ring_d.zn:
                 pl.semaphore_signal(s.epoch.at[k], inc=1, device_id=dev, device_id_type=MESH)
 
+        def give_credit(z):
+            pl.semaphore_signal(s.credit.at[z], inc=1, device_id=ring_d.core, device_id_type=MESH)
+
+        def take_credit(z):
+            pl.semaphore_wait(s.credit.at[z], 1)
+            ring_d.start(z)
+
         def epoch_wait(k):
             pl.semaphore_wait(s.epoch.at[k], 6)
+
+    plan = {}
+
+    def loop(name, n, body):
+        todo = plan.get(name, {})
+
+        def with_plan(i, carry):
+            body(i, carry)
+            for k in sorted(todo):
+
+                @pl.when(i == k)
+                def _(k=k):
+                    for act in todo[k]:
+                        act()
+
+            return 0
+
+        lax.fori_loop(0, n, with_plan, 0)
 
     def put_in(ref):
         def put(c, v):
@@ -278,14 +307,6 @@
                 s.o_qkv[:, pl.ds(pl.multiple_of(col, 128), 128)] = v[:, i * 128 : i * 128 + 128]
 
         return put
-
-    lane = lax.broadcasted_iota(jnp.int32, (128, 128), 1)
-    low_half = lane < 64
-    zero_b = jnp.zeros((), BF)
-
-    def halves(a):
-        keep = lax.broadcasted_iota(jnp.int32, a.shape, 1) < 64
-        return jnp.where(keep, a, zero_b), jnp.where(keep, zero_b, a)
 
     bounds = []
     for r in range(nrow):
@@ -298,8 +319,9 @@
         )
 
     s.bqkv[...] = jnp.zeros_like(s.bqkv)
-    s.bqkv[0:1, 0:D] = s.i_bq[...]
-    s.bqkv[0:1, 2 * D : 3 * D] = s.i_bv[...]
+    s.bqkv[0:1, 0:D] = s.i_bq[...][None, :]
+    s.bqkv[0:1, 2 * D : 3 * D] = s.i_bv[...][None, :]
+    s.bup[0:1, :] = s.i_bup[...][None, :]
     l_x.wait()
     l_q.wait()
     l_wqkv.wait()
@@ -312,62 +334,71 @@
     lax.fori_loop(0, 3 * D // 256, qkv_body, 0)
 
     scale = 0.125 * LOG2E
+    li = lax.rem(lax.broadcasted_iota(jnp.int32, (LEN, 128), 1), 64).astype(F32)
+    for r in range(nrow):
+        b0, b1 = bounds[r]
+        ti = lax.broadcasted_iota(jnp.int32, (LEN, 128), 0).astype(F32)
+        seg = jnp.where(ti >= b0, 1.0, 0.0) + jnp.where(ti >= b1, 1.0, 0.0)
+        s.koh[r * LEN : (r + 1) * LEN, :] = jnp.where(seg == li, 1.0, 0.0).astype(BF)
+        s.qoh[r * LEN : (r + 1) * LEN, :] = jnp.where(jnp.logical_or(seg == li, li >= SEGS), 0.0, -1e30).astype(BF)
+    ql = cfg.qlen
+    ti = lax.broadcasted_iota(jnp.int32, (NQ, 128), 0)
+    li = lax.rem(lax.broadcasted_iota(jnp.int32, (NQ, 128), 1), 64)
+    mine = jnp.logical_and(ti >= li * ql, ti < li * ql + ql)
+    s.koh[NP:T, :] = jnp.where(mine, 1.0, 0.0).astype(BF)
+    s.qoh[NP:T, :] = jnp.where(jnp.logical_or(mine, li * ql >= NQ), 0.0, -1e30).astype(BF)
+    one_b = jnp.ones((), BF)
+
+    def mix(h, a, b):
+        keep = lax.broadcasted_iota(jnp.int32, a.shape, 1) < 64
+        return jnp.where(keep, a, b) if h == 0 else jnp.where(keep, b, a)
+
+    def att_tile(qr, kr, cq, ck, cv, keep_e):
+        q, k, v = s.mixed[qr, cq], s.mixed[kr, ck], s.mixed[kr, cv]
+        qo, ko = s.qoh[qr, :], s.koh[kr, :]
+        o = []
+        for h in range(2):
+            sc = nt(mix(h, q, qo), mix(h, k, ko))
+            e = jnp.exp2(sc * scale - jnp.max(sc, -1, keepdims=True) * scale).astype(BF)
+            keep_e(h, e)
+            o.append(nn(e, mix(h, v, one_b)))
+        inv = pltpu.roll(1.0 / mix(1, o[0], o[1]), 64, 1)
+        s.ctx[qr, cq] = (mix(0, o[0], o[1]) * inv).astype(BF)
+        s.dctx[qr, cq] = inv.astype(BF)
+
+    def pair_cols(hp):
+        return at(hp, 128), at(hp + D // 128, 128), at(hp + 2 * D // 128, 128)
 
     def p_copy_out(i, slot):
         return pltpu.make_async_copy(s.pbuf.at[slot], s.o_p.at[i], s.psem.at[slot])
 
-    for r in range(nrow):
-        b0, b1 = bounds[r]
+    def att_body(i, _):
+        r, hp = i // (H // 2), lax.rem(i, H // 2)
+        slot = lax.rem(i, 2)
+
+        @pl.when(i >= 2)
+        def _():
+            p_copy_out(i - 2, slot).wait()
+
         for qs, ks, kw, off in TILES:
-            qi = (lax.broadcasted_iota(jnp.int32, (128, kw), 0) + qs).astype(F32)
-            ki = (lax.broadcasted_iota(jnp.int32, (128, kw), 1) + ks).astype(F32)
-            sq = jnp.where(qi >= b0, 1.0, 0.0) + jnp.where(qi >= b1, 1.0, 0.0)
-            sk = jnp.where(ki >= b0, 1.0, 0.0) + jnp.where(ki >= b1, 1.0, 0.0)
-            s.bias[:, off : off + kw] = jnp.where(sq == sk, 0.0, -1e30)
-
-        def att_body(hp, _, r=r):
-            i = r * (H // 2) + hp
-            slot = lax.rem(i, 2)
-
-            @pl.when(i >= 2)
-            def _():
-                p_copy_out(i - 2, slot).wait()
-
-            cq, ck, cv = at(hp, 128), at(hp + D // 128, 128), at(hp + 2 * D // 128, 128)
-            for qs, ks, kw, off in TILES:
-                qh = halves(s.mixed[r * LEN + qs : r * LEN + qs + 128, cq])
-                kt = s.mixed[r * LEN + ks : r * LEN + ks + kw, ck]
-                vt = s.mixed[r * LEN + ks : r * LEN + ks + kw, cv]
-                o = []
-                for h in range(2):
-                    sc = nt(qh[h], kt) * scale + s.bias[:, off : off + kw]
-                    e = jnp.exp2(sc - jnp.max(sc, -1, keepdims=True))
-                    p = (e * (1.0 / jnp.sum(e, -1, keepdims=True))).astype(BF)
-                    s.pbuf[slot, h, :, off : off + kw] = p
-                    o.append(nn(p, vt))
-                s.ctx[r * LEN + qs : r * LEN + qs + 128, cq] = jnp.where(low_half, o[0], o[1]).astype(BF)
-            p_copy_out(i, slot).start()
-            return 0
-
-        lax.fori_loop(0, H // 2, att_body, 0)
-
-    qi = lax.broadcasted_iota(jnp.int32, (NQ, NQ), 0)
-    ki = lax.broadcasted_iota(jnp.int32, (NQ, NQ), 1)
-    ql = cfg.qlen
-    qbias = jnp.where((qi // ql) == (ki // ql), 0.0, -1e30)
-    for hp in range(H // 2):
-        cq = slice(hp * 128, hp * 128 + 128)
-        qh = halves(s.mixed[NP:T, hp * 128 : hp * 128 + 128])
-        kt = s.mixed[NP:T, D + hp * 128 : D + hp * 128 + 128]
-        vt = s.mixed[NP:T, 2 * D + hp * 128 : 2 * D + hp * 128 + 128]
-        o = []
-        for h in range(2):
-            sc = nt(qh[h], kt) * scale + qbias
-            e = jnp.exp2(sc - jnp.max(sc, -1, keepdims=True))
-            p = (e * (1.0 / jnp.sum(e, -1, keepdims=True))).astype(BF)
-            s.pq[hp, h] = p
-            o.append(nn(p, vt))
-        s.ctx[NP:T, cq] = jnp.where(low_half, o[0], o[1]).astype(BF)
+
+            def keep_e(h, e):
+                s.pbuf[slot, h, :, off : off + kw] = e
+
+            att_tile(rows_at(r * LEN + qs, 128, 128), rows_at(r * LEN + ks, kw, 128), *pair_cols(hp), keep_e)
+        p_copy_out(i, slot).start()
+        return 0
+
+    lax.fori_loop(0, nrow * (H // 2), att_body, 0)
+
+    def att_q_body(hp, _):
+        def keep_e(h, e):
+            s.pq[hp, h] = e
+
+        att_tile(slice(NP, T), slice(NP, T), *pair_cols(hp), keep_e)
+        return 0
+
+    lax.fori_loop(0, H // 2, att_q_body, 0)
     last = nrow * (H // 2)
     p_copy_out(last - 2, (last - 2) % 2).wait()
     p_copy_out(last - 1, (last - 1) % 2).wait()
@@ -376,11 +407,11 @@
 
     def out_body(t, _):
         rr = at(t, TT)
-        v = nn(s.ctx[rr, :], s.wout[...]) + s.i_bout[...] + s.x[rr, :].astype(F32)
+        v = nn(s.ctx[rr, :], s.wout[...]) + v_bout[...] + s.x[rr, :].astype(F32)
         y, inv = norm_stats(v)
         s.y1[rr, :] = y.astype(BF)
         s.st[rr, 0:1] = inv
-        s.fb[rr, :] = (y * s.i_g1[...] + s.i_b1[...]).astype(BF)
+        s.fb[rr, :] = (y * v_g1[...] + v_b1[...]).astype(BF)
         return 0
 
     lax.fori_loop(0, T // TT, out_body, 0)
@@ -391,7 +422,7 @@
         c = at(n, 256)
         for m in range(T // TT):
             rr = slice(m * TT, m * TT + TT)
-            h = nn(s.fb[rr, :], s.wup[:, c]) + s.i_bup[:, c]
+            h = nn(s.fb[rr, :], s.wup[:, c]) + s.bup[0:1, c]
             cdf = 0.5 * (1.0 + lax.erf(h * 0.7071067811865476))
             s.hid[rr, c] = (h * cdf).astype(BF)
             s.slo[rr, c] = (cdf + h * jnp.exp2(h * h * (-0.5 * LOG2E)) * 0.3989422804014327).astype(BF)
@@ -404,12 +435,12 @@
 
     def down_body(t, _):
         rr = at(t, TT)
-        first = s.y1[rr, :].astype(F32) * s.i_g1[...] + s.i_b1[...]
-        v = first + (nn(s.hid[rr, :], s.wdn[...]) + s.i_bdn[...])
+        first = s.y1[rr, :].astype(F32) * v_g1[...] + v_b1[...]
+        v = first + (nn(s.hid[rr, :], s.wdn[...]) + v_bdn[...])
         y, inv = norm_stats(v)
         s.gs[rr, :] = y
         s.st[rr, 1:2] = inv
-        sec = (y * s.i_g2[...] + s.i_b2[...]).astype(BF)
+        sec = (y * v_g2[...] + v_b2[...]).astype(BF)
         s.gb[rr, :] = sec
         pj = nn(sec, s.wproj[...])
         il = lax.rsqrt(jnp.sum(pj * pj, -1, keepdims=True) + 1e-06)
@@ -485,7 +516,9 @@
     mid = line.astype(BF)
     lo = (line - mid.astype(F32)).astype(BF)
     s.lg[0, 0:nq_all, :] = nn(sel, hi) + (nn(sel, mid) + nn(sel, lo))
-    s.lg[0, nq_all : 2 * nq_all, 0:slots] = s.i_teach[...]
+    s.tsq[...] = jnp.zeros_like(s.tsq)
+    s.tsq[0:slots, 0:nq_all] = s.i_teach[...]
+    s.lg[0, nq_all : 2 * nq_all, :] = s.tsq[...].T[0:nq_all, :]
     l_copies = []
     for k in range(1, n_psg):
         c = remote(
@@ -562,6 +595,47 @@
 
     s.misc[:, 0:128] = tn(s.gb[...], s.gp[...]).astype(BF)
 
+    if sums:
+        al = (0, 1, 2, 3)
+
+        def at_step(name, k, f, *args):
+            plan.setdefault(name, {}).setdefault(k, []).append(lambda: f(*args))
+
+        for z in range(4):
+            at_step("ff", 3 * z + 2, give_credit, z)
+        for z in range(3):
+            at_step("ff", 3 * z + 3, take_credit, z)
+        at_step("norm1", 2, ring_d.to_b, 0, 1)
+        at_step("gup", 6, ring_d.to_b, 2, 3)
+        at_step("gout", 0, ring_d.to_z, 0, 1)
+        at_step("gout", 2, ring_d.to_z, 2, 3)
+        at_step("att0", 1, ring_u.to_b, 0, 1)
+        at_step("att0", 1, ring_o.to_a, *al)
+        at_step("att0", 3, ring_u.to_b, 2, 3)
+        at_step("att1", 0, ring_d.to_core)
+        at_step("att1", 0, ring_1.to_a, *al)
+        at_step("att1", 1, ring_u.to_z, 0, 1)
+        at_step("att1", 1, ring_o.to_b, *al)
+        at_step("att1", 2, ring_u.to_z, 2, 3)
+        at_step("att1", 2, ring_d.out, put_in(s.o_dn))
+        at_step("att1", 3, ring_o.to_z, *al)
+        at_step("att1", 3, ring_1.to_b, *al)
+        at_step("att2", 0, ring_2.to_a, *al)
+        at_step("att2", 1, ring_1.to_z, *al)
+        at_step("att2", 2, ring_u.to_core)
+        at_step("att2", 2, ring_o.to_core)
+        at_step("att2", 2, ring_2.to_b, *al)
+        at_step("att2", 3, ring_u.out, put_in(s.o_up))
+        at_step("att2", 3, ring_o.out, put_in(s.o_out))
+        at_step("att2", 3, ring_1.to_core)
+        at_step("dx", 0, ring_3.to_a, *al)
+        at_step("dx", 0, ring_m.to_a, *al)
+        at_step("dx", 0, ring_2.to_z, *al)
+        at_step("dx", 1, ring_1.out, put_group(0))
+        at_step("dx", 2, ring_3.to_b, *al)
+        at_step("dx", 2, ring_m.to_b, *al)
+        at_step("dx", 3, ring_2.to_core)
+
     s.vr[...] = jnp.zeros_like(s.vr)
 
     def addrow(k, v):
@@ -573,7 +647,7 @@
         y = s.gs[rr, :]
         addrow(6, g * y)
         addrow(7, g)
-        d = g * s.i_g2[...]
+        d = g * v_g2[...]
         gs = s.st[rr, 1:2] * (d - jnp.mean(d, -1, keepdims=True) - y * jnp.mean(d * y, -1, keepdims=True))
         s.gs[rr, :] = gs
         b = gs.astype(BF)
@@ -581,7 +655,7 @@
         addrow(5, b.astype(F32))
         return 0
 
-    lax.fori_loop(0, T // TT, norm2_body, 0)
+    loop('norm2', T // TT, norm2_body)
 
     def ff_body(n, _):
         c = at(n, 256)
@@ -596,10 +670,12 @@
         s.wdn[c, :] = tn(s.hid[:, c], s.gb[...]).astype(BF)
         return 0
 
-    lax.fori_loop(0, FF // 256, ff_body, 0)
-
+    loop('ff', FF // 256, ff_body)
     if sums:
         epoch_signal(0)
+        take_credit(3)
+        epoch_wait(0)
+        ring_d.to_a(*al)
 
     def norm1_body(t, _):
         rr = at(t, TT)
@@ -607,7 +683,7 @@
         y = s.y1[rr, :].astype(F32)
         addrow(3, g * y)
         addrow(4, g)
-        d = g * s.i_g1[...]
+        d = g * v_g1[...]
         gs = s.st[rr, 0:1] * (d - jnp.mean(d, -1, keepdims=True) - y * jnp.mean(d * y, -1, keepdims=True))
         s.gs[rr, :] = gs
         b = gs.astype(BF)
@@ -615,38 +691,36 @@
         addrow(2, b.astype(F32))
         return 0
 
-    lax.fori_loop(0, T // TT, norm1_body, 0)
+    loop('norm1', T // TT, norm1_body)
 
     def gup_body(n, _):
         c = at(n, 256)
         s.wup[:, c] = tn(s.fb[...], s.slo[:, c]).astype(BF)
         return 0
 
-    if sums:
-        epoch_wait(0)
-        ring_d.step1()
-    lax.fori_loop(0, FF // 512, gup_body, 0)
-    if sums:
-        ring_d.step2()
-    lax.fori_loop(FF // 512, FF // 256, gup_body, 0)
+    loop('gup', FF // 256, gup_body)
     if sums:
         epoch_signal(1)
-        ring_d.step3()
+        epoch_wait(1)
+        ring_u.start(*al)
 
     def dctx_body(t, _):
         rr = at(t, TT)
-        s.dctx[rr, :] = nt(s.gb[rr, :], s.wout[...]).astype(BF)
-        return 0
-
-    lax.fori_loop(0, T // TT, dctx_body, 0)
+        s.dctx[rr, :] = (nt(s.gb[rr, :], s.wout[...]) * s.dctx[rr, :].astype(F32)).astype(BF)
+        return 0
+
+    loop('dctx', T // TT, dctx_body)
     if sums:
-        ring_d.step4()
-        epoch_wait(1)
-        ring_u.step1()
-    s.wout[...] = tn(s.ctx[...], s.gb[...]).astype(BF)
+        ring_u.to_a(*al)
+
+    def gout_body(n, _):
+        c = at(n, 256)
+        s.wout[:, c] = tn(s.ctx[...], s.gb[:, c]).astype(BF)
+        return 0
+
+    loop('gout', D // 256, gout_body)
     if sums:
-        ring_o.step1()
-        ring_d.step5()
+        ring_o.start(*al)
 
     def p_copy_in(j):
         g, rest = j // (2 * nrow), lax.rem(j, 2 * nrow)
@@ -657,6 +731,16 @@
     steps = nrow * (H // 2)
     p_copy_in(0).start()
 
+    def back_tile(qr, kr, cq, ck, cv, e_of, keep_ds):
+        do, k, v = s.dctx[qr, cq], s.mixed[kr, ck], s.mixed[kr, cv]
+        prod = (-pltpu.roll(do.astype(F32) * s.ctx[qr, cq].astype(F32), 64, 1)).astype(BF)
+        dq = []
+        for h in range(2):
+            ds = (e_of(h).astype(F32) * nt(mix(h, do, prod), mix(h, v, one_b))).astype(BF)
+            keep_ds(h, ds)
+            dq.append(nn(ds, k))
+        return (mix(0, dq[0], dq[1]) * 0.125).astype(BF)
+
     def att_back(j, _):
         g, rest = j // (2 * nrow), lax.rem(j, 2 * nrow)
         r = rest // 2
@@ -668,25 +752,20 @@
             p_copy_in(j + 1).start()
 
         p_copy_in(j).wait()
-        cq, ck, cv = at(hp, 128), at(hp + D // 128, 128), at(hp + 2 * D // 128, 128)
+        cq, ck, cv = pair_cols(hp)
         base = r * LEN
 
         def rws(a, n):
-            return pl.ds(pl.multiple_of(base + a, 128), n)
+            return rows_at(base + a, n, 128)
 
         for qs, ks, kw, off in TILES:
-            do = halves(s.dctx[rws(qs, 128), cq])
-            kt = s.mixed[rws(ks, kw), ck]
-            vt = s.mixed[rws(ks, kw), cv]
-            dq = []
-            for h in range(2):
-                p = s.pbuf[slot, h, :, off : off + kw].astype(F32)
-                dp = nt(do[h], vt)
-                pd = p * dp
-                ds = (pd - p * jnp.sum(pd, -1, keepdims=True)).astype(BF)
+
+            def keep_ds(h, ds):
                 s.ds[h, :, off : off + kw] = ds
-                dq.append(nn(ds, kt))
-            s.dq[qs : qs + 128, :] = (jnp.where(low_half, dq[0], dq[1]) * 0.125).astype(BF)
+
+            s.dq[qs : qs + 128, :] = back_tile(
+                rws(qs, 128), rws(ks, kw), cq, ck, cv, lambda h: s.pbuf[slot, h, :, off : off + kw], keep_ds
+            )
         for kk in range(4):
             dk = [None, None]
             dv = [None, None]
@@ -701,94 +780,48 @@
                     b = tn(s.pbuf[slot, h, :, off + rel : off + rel + 128], ot)
                     dk[h] = a if dk[h] is None else dk[h] + a
                     dv[h] = b if dv[h] is None else dv[h] + b
-            s.dk[kk * 128 : kk * 128 + 128, :] = (jnp.where(low_half, dk[0], dk[1]) * 0.125).astype(BF)
-            s.dv[kk * 128 : kk * 128 + 128, :] = jnp.where(low_half, dv[0], dv[1]).astype(BF)
+            s.dk[kk * 128 : kk * 128 + 128, :] = (mix(0, dk[0], dk[1]) * 0.125).astype(BF)
+            s.dv[kk * 128 : kk * 128 + 128, :] = mix(0, dv[0], dv[1]).astype(BF)
         s.mixed[rws(0, LEN), cq] = s.dq[...]
         s.mixed[rws(0, LEN), ck] = s.dk[...]
         s.mixed[rws(0, LEN), cv] = s.dv[...]
         return 0
 
     def att_back_q(hp, _):
-        cq, ck, cv = at(hp, 128), at(hp + D // 128, 128), at(hp + 2 * D // 128, 128)
-        qt = s.mixed[NP:T, cq]
-        kt = s.mixed[NP:T, ck]
-        vt = s.mixed[NP:T, cv]
-        ot = s.dctx[NP:T, cq]
-        do = halves(ot)
-        dq, dk, dv = [], [], []
-        for h in range(2):
-            pb = s.pq[hp, h]
-            p = pb.astype(F32)
-            pd = p * nt(do[h], vt)
-            ds = (pd - p * jnp.sum(pd, -1, keepdims=True)).astype(BF)
-            dq.append(nn(ds, kt))
-            dk.append(tn(ds, qt))
-            dv.append(tn(pb, ot))
-        s.mixed[NP:T, cq] = (jnp.where(low_half, dq[0], dq[1]) * 0.125).astype(BF)
-        s.mixed[NP:T, ck] = (jnp.where(low_half, dk[0], dk[1]) * 0.125).astype(BF)
-        s.mixed[NP:T, cv] = jnp.where(low_half, dv[0], dv[1]).astype(BF)
+        cq, ck, cv = pair_cols(hp)
+        rr = slice(NP, T)
+        q, do = s.mixed[rr, cq], s.dctx[rr, cq]
+        grads = [None, None]
+
+        def keep_ds(h, ds):
+            grads[h] = ds
+
+        dq = back_tile(rr, rr, cq, ck, cv, lambda h: s.pq[hp, h], keep_ds)
+        dk = [tn(grads[h], q) for h in range(2)]
+        dv = [tn(s.pq[hp, h], do) for h in range(2)]
+        s.mixed[rr, cq] = dq
+        s.mixed[rr, ck] = (mix(0, dk[0], dk[1]) * 0.125).astype(BF)
+        s.mixed[rr, cv] = mix(0, dv[0], dv[1]).astype(BF)
         return 0
 
     lax.fori_loop(0, H // 2, att_back_q, 0)
 
-    groups = (s.ctx, s.fb, s.gb)
+    groups = (s.fb, s.gb, s.ctx)
 
     def group_grad(g):
         for w in range(3):
             c = w * D + g * 256
             groups[g][0:D, w * 256 : w * 256 + 256] = tn(s.x[...], s.mixed[:, c : c + 256]).astype(BF)
 
-    def step(j, _):
-        att_back(j, 0)
+    for g in range(3):
+
+        @functools.partial(loop, 'att%d' % g, 2 * nrow)
+        def _(j, _, g=g):
+            att_back(2 * nrow * g + j, 0)
+
+        group_grad(g)
         if sums:
-
-            @pl.when(j == 1)
-            def _():
-                ring_u.step2()
-                ring_o.step2()
-
-            @pl.when(j == 2)
-            def _():
-                ring_d.step6(put_in(s.o_dn))
-
-        @pl.when(j == 3)
-        def _():
-            group_grad(0)
-            if sums:
-                ring_1.step1()
-
-        if sums:
-
-            @pl.when(j == 5)
-            def _():
-                ring_u.step3()
-                ring_o.step3()
-                ring_1.step2()
-
-        @pl.when(j == 7)
-        def _():
-            group_grad(1)
-            if sums:
-                ring_2.step1()
-                ring_u.step4()
-                ring_o.step4()
-                ring_1.step3()
-
-        if sums:
-
-            @pl.when(j == 9)
-            def _():
-                ring_u.step5()
-                ring_o.step5()
-                ring_1.step4()
-                ring_2.step2()
-
-        return 0
-
-    lax.fori_loop(0, steps, step, 0)
-    group_grad(2)
-    if sums:
-        ring_3.step1()
+            (ring_1, ring_2, ring_3)[g].start(*al)
     for w, k in ((0, 0), (2, 1)):
         s.vr[k : k + 1, :] = jnp.sum(s.mixed[:, w * D : w * D + D].astype(F32), axis=0, keepdims=True)
 
@@ -810,24 +843,14 @@
                     v = jnp.where(lane == 8 + k, s.tcol[(4 * d + k) * q : (4 * d + k) * q + q, :], v)
                 s.vcol[rr, :] = v
         s.misc[:, 128:256] = s.vcol[...].astype(BF)
-        ring_m.step1()
-        ring_u.step6(put_in(s.o_up))
-        ring_o.step6(put_in(s.o_out))
-        ring_1.step5()
-        ring_2.step3()
+        ring_m.start(*al)
 
     def dx_body(t, _):
         rr = at(t, TT)
         s.gs[rr, :] = s.gs[rr, :] + nt(s.mixed[rr, :], s.wqkv[...])
         return 0
 
-    lax.fori_loop(0, T // TT // 2, dx_body, 0)
-    if sums:
-        ring_3.step2()
-        ring_m.step2()
-        ring_2.step4()
-        ring_1.step6(put_group(0))
-    lax.fori_loop(T // TT // 2, T // TT, dx_body, 0)
+    loop('dx', T // TT, dx_body)
     outs = [
         pltpu.make_async_copy(s.gs.at[0:NP], s.o_gp, s.osem.at[2]),
         pltpu.make_async_copy(s.gs.at[NP:T], s.o_gq, s.osem.at[3]),
@@ -847,16 +870,13 @@
     for c in outs:
         c.start()
     if sums:
-        ring_3.step3()
-        ring_m.step3()
-        ring_2.step5()
-        ring_3.step4()
-        ring_m.step4()
-        ring_2.step6(put_group(1))
-        ring_3.step5()
-        ring_m.step5()
-        ring_3.step6(put_group(2))
-        ring_m.step6(put_in(s.o_misc))
+        ring_3.to_z(*al)
+        ring_m.to_z(*al)
+        ring_2.out(put_group(1))
+        ring_3.to_core()
+        ring_m.to_core()
+        ring_3.out(put_group(2))
+        ring_m.out(put_in(s.o_misc))
         for r in rings:
             r.finish()
     for c in q_copies + l_copies + g_copies + loss_copies:
@@ -869,6 +889,65 @@
         s.o_loss[...] = s.ls[0]
     for c in [o_pe, o_qe] + outs:
         c.wait()
+
+
+def finish_kernel(names, *refs):
+    s = Space()
+    for name, ref in zip(names, refs):
+        setattr(s, name, ref)
+    pairs = ((s.pe, s.o_pe), (s.qe, s.o_qe), (s.gp, s.o_gp), (s.gq, s.o_gq))
+    pairs += ((s.dn, s.o_dn), (s.up, s.o_up), (s.out, s.o_out), (s.qkv, s.o_qkv))
+    ways = []
+    for (src, dst), buf in zip(pairs, (s.bpe, s.bqe, s.bgp, s.bgq, s.bdn, s.bup, s.bout, s.bqkv)):
+        n = src.shape[0] // 4 if src.shape[0] > 512 else src.shape[0]
+        for i in range(src.shape[0] // n):
+            k = len(ways)
+            rr = slice(i * n, i * n + n)
+            ways.append(
+                (
+                    pltpu.make_async_copy(src.at[rr], buf.at[rr], s.sem.at[0, k]),
+                    pltpu.make_async_copy(buf.at[rr], dst.at[rr], s.sem.at[1, k]),
+                )
+            )
+    for c, _ in ways:
+        c.start()
+    s.o_loss[...] = s.loss[0, 0]
+    s.o_proj[...] = s.misc[:, 0:128]
+    q = s.misc.shape[0]
+    s.sq[...] = jnp.zeros_like(s.sq)
+    s.sq[0:q, :] = s.misc[:, 128:256]
+    s.sq[...] = s.sq[...].T
+    for k in range(8):
+        getattr(s, "o_v%d" % k)[...] = s.sq[k, 0:q]
+    s.o_bup[...] = jnp.concatenate([s.sq[8 + k : 9 + k, 0:q] for k in range(4)], 1)[0]
+    for c, d in ways:
+        c.wait()
+        d.start()
+    for _, d in ways:
+        d.wait()
+
+
+def finish(o):
+    sd = jax.ShapeDtypeStruct
+    any_spec = pl.BlockSpec(memory_space=pl.ANY)
+    vm = pl.BlockSpec(memory_space=pltpu.VMEM)
+    names = ["pe", "qe", "gp", "gq", "dn", "up", "out", "qkv"]
+    ins = [(n, o["o_" + n], any_spec) for n in names] + [("loss", o["o_loss"], vm), ("misc", o["o_misc"], vm)]
+    outs = [("o_" + n, sd(o["o_" + n].shape, o["o_" + n].dtype), any_spec) for n in names]
+    q = o["o_misc"].shape[0]
+    outs += [("o_loss", sd((), F32), pl.BlockSpec(memory_space=pltpu.SMEM)), ("o_proj", sd((q, 128), F32), vm)]
+    outs += [("o_v%d" % k, sd((q,), F32), vm) for k in range(8)] + [("o_bup", sd((4 * q,), F32), vm)]
+    scratch = [("sq", pltpu.VMEM((128, 128), F32)), ("sem", pltpu.SemaphoreType.DMA((2, 14)))]
+    scratch += [("b" + n, pltpu.VMEM(o["o_" + n].shape, o["o_" + n].dtype)) for n in names]
+    all_names = [n for n, *_ in ins] + [n for n, *_ in outs] + [n for n, _ in scratch]
+    res = pl.pallas_call(
+        functools.partial(finish_kernel, all_names),
+        out_shape=[v[1] for v in outs],
+        in_specs=[v[2] for v in ins],
+        out_specs=[v[2] for v in outs],
+        scratch_shapes=[v for _, v in scratch],
+    )(*[v[1] for v in ins])
+    return dict(zip([n for n, *_ in outs], res))
 
 
 def make_body(n_dp, n_psg):
@@ -892,25 +971,24 @@
         npair = rows * (H // 2)
         any_spec = pl.BlockSpec(memory_space=pl.ANY)
         vm = pl.BlockSpec(memory_space=pltpu.VMEM)
-        row = lambda v: v.reshape(1, -1)
         ins = [
             ("i_pass", passage_states.reshape(NP, D), any_spec),
             ("i_query", query_states.reshape(NQ, D), any_spec),
             ("i_seg", segment_ids, vm),
-            ("i_teach", teacher_scores, vm),
+            ("i_teach", teacher_scores.T, vm),
             ("i_wqkv", w_qkv, any_spec),
-            ("i_bq", row(bias_q), vm),
-            ("i_bv", row(bias_v), vm),
+            ("i_bq", bias_q, vm),
+            ("i_bv", bias_v, vm),
             ("i_wout", w_out, any_spec),
-            ("i_bout", row(bias_out), vm),
-            ("i_g1", row(ln1_gain), vm),
-            ("i_b1", row(ln1_bias), vm),
+            ("i_bout", bias_out, vm),
+            ("i_g1", ln1_gain, vm),
+            ("i_b1", ln1_bias, vm),
             ("i_wup", w_up, any_spec),
-            ("i_bup", row(bias_up), vm),
+            ("i_bup", bias_up, vm),
             ("i_wdn", w_down, any_spec),
-            ("i_bdn", row(bias_down), vm),
-            ("i_g2", row(ln2_gain), vm),
-            ("i_b2", row(ln2_bias), vm),
+            ("i_bdn", bias_down, vm),
+            ("i_g2", ln2_gain, vm),
+            ("i_b2", ln2_bias, vm),
             ("i_wproj", w_proj, any_spec),
         ]
         sd = jax.ShapeDtypeStruct
@@ -951,10 +1029,13 @@
             ("wdn", V((FF, D), BF)),
             ("wproj", V((D, E), BF)),
             ("bqkv", V((8, 3 * D), F32)),
+            ("vin", V((8, D), F32)),
+            ("tsq", V((128, 128), F32)),
             ("mixed", V((T, 3 * D), BF)),
             ("pbuf", V((2, 2, 128, PW), BF)),
             ("pq", V((H // 2, 2, NQ, NQ), BF)),
-            ("bias", V((128, PW), F32)),
+            ("koh", V((T, 128), BF)),
+            ("qoh", V((T, 128), BF)),
             ("ctx", V((T, D), BF)),
             ("y1", V((T, D), BF)),
             ("fb", V((T, D), BF)),
@@ -1009,6 +1090,7 @@
                 ("rm", V((b // 2, 128), F32)),
                 ("gss", DMA((7, 18))),
                 ("grs", DMA((7, 18))),
+                ("credit", pltpu.SemaphoreType.REGULAR((4,))),
                 ("epoch", pltpu.SemaphoreType.REGULAR((2,))),
             ]
         cfg.names = [a for a, *_ in ins] + [a for a, *_ in outs] + [a for a, _ in scratch]
@@ -1023,7 +1105,11 @@
             ),
         )(*[i[1] for i in ins])
         o = dict(zip([a for a, *_ in outs], res))
-        loss = o["o_loss"][0, 0]
+        if cfg.sums:
+            o = finish(o)
+            loss = o["o_loss"]
+        else:
+            loss = o["o_loss"][0, 0]
         if not cfg.loss_here:
             loss = lax.psum(loss, "dp")
         head = (
@@ -1034,10 +1120,10 @@
             o["o_gq"].reshape(qn, ql, D),
         )
         if cfg.sums:
-            m = o["o_misc"]
-            vec = [m[:, 128 + k] for k in range(8)]
-            g_bup = m[:, 136:140].T.reshape(-1)
-            g_qkv, g_out, g_up, g_dn, g_proj = o["o_qkv"], o["o_out"], o["o_up"], o["o_dn"], m[:, 0:128]
+            vec = [o["o_v%d" % k] for k in range(8)]
+            g_qkv, g_out, g_up, g_bup, g_dn, g_proj = [
+                o["o_" + k] for k in ("qkv", "out", "up", "bup", "dn", "proj")
+            ]
         else:
             q3 = o["o_q"].reshape(3, D, 3, 256)
             q3 = jnp.transpose(q3, (1, 2, 0, 3)).reshape(D, 3 * D)

time: 257 us -> 198 us (0.77)
  Pallas kernels: 227 us -> 197 us
  local copies, waits for them, and re-layouts: 27.9 us -> 0 us
    pallas_call x1, Pallas kernels: 227 us -> 192 us  [body(): pl.pallas_call(functools.partial(kernel, cfg), out_shape=[o[1] for o in o...]
    unnamed x19 -> x0, local copies, waits for them, and re-layouts: 11.7 us -> none
    reshape x9 -> x0, local copies, waits for them, and re-layouts: 10.7 us -> none  [the longest x8 10.1 us: body(): row = lambda v: v.reshape(1, -1)]
    pallas_call x0 -> x1, Pallas kernels: none -> 5.42 us  [finish(): pl.pallas_call(functools.partial(finish_kernel, all_names), out_shape=[v[...]
    slice x3 -> x0, local copies, waits for them, and re-layouts: 4.6 us -> none  [the longest x1 2.06 us: body(): vec = [m[:, 128 + k] for k in range(8)]]
where the time goes in v2:
time: 198 us
  Pallas kernels  197 us (99%)
    pallas_call x1, Pallas kernels, body(): pl.pallas_call(functools.partial(kernel, cfg), out_shape=[o[1] for o in o...  192 us
    pallas_call x1, Pallas kernels, finish(): pl.pallas_call(functools.partial(finish_kernel, all_names), out_shape=[v[...  5.42 us

profile of v2, /device:TPU:1, one launch (start us, length us, event | category | flops | bytes accessed | tf_op | source)
XLA Modules:
  0.0 197.8 jit_solution(6919114104868443729)
XLA Ops:
  0.7 191.6 %shard_map.321 = (bf16[1024,128]{1,0:T(8,128)(2,1)}, bf16[128,128]{1,0:T(8,128)(2,1)}, f32[8,128]{1,0:T(8,128)}, f32[1024,768]{1,0:T(8,128)}, f32[128,768]{1,0:T...) custom-call(bf16[1024,768]{1,0:T(8,128)(2,1)} %bitcast.7, ...), custom_call_target="tpu_custom_call" | custom-call | tf_op jit(solution)/shard_map/pallas_call | solution.py:1097
  192.2 5.4 %shard_map.322 = (bf16[1024,128]{1,0:T(8,128)(2,1)}, bf16[128,128]{1,0:T(8,128)(2,1)}, f32[1024,768]{1,0:T(8,128)}, f32[128,768]{1,0:T(8,128)}, f32[96,768]{1,0:...) custom-call(bf16[1024,128]{1,0:T(8,128)(2,1)} %get-tuple-element.48., ...), custom_call_target="tpu_custom_call" | custom-call | tf_op jit(solution)/shard_map/pallas_call | solution.py:943

commit v3 on v2

--- a/solution.py
+++ b/solution.py
@@ -97,6 +97,20 @@
         z = lax.rem(self.z + k + 1, 4)
         return self.remote(14 + k, self.part(4 * z + 2 * self.x + self.y, 1, self.c), self.z_at(k), self.zn[k])
 
+    def send_z(self, z):
+        k = lax.rem(z - self.z + 3, 4)
+
+        @pl.when(z != self.z)
+        def _():
+            self.s_z(z, k).start()
+
+    def s_z(self, z, k):
+        return pltpu.make_async_remote_copy(
+            src_ref=self.part(4 * z + 2 * self.x + self.y, 1, self.c), dst_ref=self.z_at(k),
+            send_sem=self.s.gss.at[self.u, 14 + k], recv_sem=self.s.grs.at[self.u, 14 + k],
+            device_id={"dp": z * 2 + self.x}, device_id_type=MESH,
+        )
+
     def copy_d(self):
         h = self.b // 2
         src = self.f.at[pl.ds(pl.multiple_of((1 - self.c) * h, 8), h), :]
@@ -131,9 +145,7 @@
         for z in zs:
             self.copy_b(z).wait_recv()
             self.add(self.part(4 * z + 2 * self.x + self.y, 1, self.c), self.b_at(z))
-        if zs[-1] == 3:
-            for k in range(3):
-                self.copy_z(k).start()
+            self.send_z(z)
 
     def to_core(self):
         v = self.part(4 * self.z + 2 * self.x + self.y, 1, self.c)[...].astype(F32)
@@ -163,6 +175,8 @@
 def place(ref, f, n, width):
     def ref_at(i, x=0, m=1):
         row, col = f(i)
+        if not isinstance(row, int):
+            return ref.at[pl.ds(pl.multiple_of(row, 16), n), col : col + width]
         return ref.at[row + x * n : row + x * n + m * n, col : col + width]
 
     return ref_at
@@ -180,12 +194,12 @@
     )
     down = (
         place(s.hid, lambda z: (0, z * h), 4 * e, h),
-        place(s.hid, lambda z: (2 * e * (z % 2), (4 + z // 2) * h), e, h),
+        place(s.arecv, lambda z: (2 * e * z, 0), e, h),
         place(s.hid, lambda z: (e * z, 6 * h), e, h),
         place(s.hid, lambda z: (e * z, 7 * h), e, h),
     )
     up = (
-        place(s.slo, lambda z: (4 * b * z, 0), 4 * b, w),
+        place(s.hid, lambda z: (4 * b * z, 0), 4 * b, w),
         place(s.slo, lambda z: (2 * b * z, w), b, w),
         place(s.slo, lambda z: (b * (8 + z), w), b, w),
         place(s.slo, lambda z: (b * (12 + z), w), b, w),
@@ -233,7 +247,8 @@
 
     def load(k, src, dst):
         c = pltpu.make_async_copy(src, dst, s.lsem.at[k])
-        c.start()
+        if k < 3:
+            c.start()
         return c
 
     l_x = load(0, s.i_pass, s.x.at[0:NP])
@@ -272,6 +287,10 @@
             pl.semaphore_wait(s.credit.at[z], 1)
             ring_d.start(z)
 
+        def start_up():
+            pl.semaphore_wait(s.credit.at[4], 1)
+            ring_u.start(0, 1, 2, 3)
+
         def epoch_wait(k):
             pl.semaphore_wait(s.epoch.at[k], 6)
 
@@ -325,6 +344,8 @@
     l_x.wait()
     l_q.wait()
     l_wqkv.wait()
+    for c in (l_wout, l_wup, l_wdn, l_wpj):
+        c.start()
 
     def qkv_body(n, _):
         c = at(n, 256)
@@ -334,37 +355,45 @@
     lax.fori_loop(0, 3 * D // 256, qkv_body, 0)
 
     scale = 0.125 * LOG2E
-    li = lax.rem(lax.broadcasted_iota(jnp.int32, (LEN, 128), 1), 64).astype(F32)
+    li = lax.broadcasted_iota(jnp.int32, (LEN, 128), 1).astype(F32)
+    si = lax.broadcasted_iota(jnp.int32, (128, LEN), 0).astype(F32)
     for r in range(nrow):
         b0, b1 = bounds[r]
+        rr = slice(r * LEN, (r + 1) * LEN)
         ti = lax.broadcasted_iota(jnp.int32, (LEN, 128), 0).astype(F32)
         seg = jnp.where(ti >= b0, 1.0, 0.0) + jnp.where(ti >= b1, 1.0, 0.0)
-        s.koh[r * LEN : (r + 1) * LEN, :] = jnp.where(seg == li, 1.0, 0.0).astype(BF)
-        s.qoh[r * LEN : (r + 1) * LEN, :] = jnp.where(jnp.logical_or(seg == li, li >= SEGS), 0.0, -1e30).astype(BF)
+        s.koh[rr, :] = jnp.where(seg == li, 1.0, 0.0).astype(BF)
+        ti = lax.broadcasted_iota(jnp.int32, (128, LEN), 1).astype(F32)
+        seg = jnp.where(ti >= b0, 1.0, 0.0) + jnp.where(ti >= b1, 1.0, 0.0)
+        s.qoh[:, rr] = jnp.where(jnp.logical_or(seg == si, si >= SEGS), 0.0, -1e30).astype(BF)
     ql = cfg.qlen
     ti = lax.broadcasted_iota(jnp.int32, (NQ, 128), 0)
-    li = lax.rem(lax.broadcasted_iota(jnp.int32, (NQ, 128), 1), 64)
-    mine = jnp.logical_and(ti >= li * ql, ti < li * ql + ql)
-    s.koh[NP:T, :] = jnp.where(mine, 1.0, 0.0).astype(BF)
-    s.qoh[NP:T, :] = jnp.where(jnp.logical_or(mine, li * ql >= NQ), 0.0, -1e30).astype(BF)
-    one_b = jnp.ones((), BF)
-
-    def mix(h, a, b):
-        keep = lax.broadcasted_iota(jnp.int32, a.shape, 1) < 64
-        return jnp.where(keep, a, b) if h == 0 else jnp.where(keep, b, a)
-
-    def att_tile(qr, kr, cq, ck, cv, keep_e):
-        q, k, v = s.mixed[qr, cq], s.mixed[kr, ck], s.mixed[kr, cv]
-        qo, ko = s.qoh[qr, :], s.koh[kr, :]
-        o = []
-        for h in range(2):
-            sc = nt(mix(h, q, qo), mix(h, k, ko))
-            e = jnp.exp2(sc * scale - jnp.max(sc, -1, keepdims=True) * scale).astype(BF)
-            keep_e(h, e)
-            o.append(nn(e, mix(h, v, one_b)))
-        inv = pltpu.roll(1.0 / mix(1, o[0], o[1]), 64, 1)
-        s.ctx[qr, cq] = (mix(0, o[0], o[1]) * inv).astype(BF)
-        s.dctx[qr, cq] = inv.astype(BF)
+    li = lax.broadcasted_iota(jnp.int32, (NQ, 128), 1)
+    s.koh[NP:T, :] = jnp.where(jnp.logical_and(ti >= li * ql, ti < li * ql + ql), 1.0, 0.0).astype(BF)
+    si = lax.broadcasted_iota(jnp.int32, (128, NQ), 0)
+    ti = lax.broadcasted_iota(jnp.int32, (128, NQ), 1)
+    mine = jnp.logical_and(ti >= si * ql, ti < si * ql + ql)
+    s.qoh[:, NP:T] = jnp.where(jnp.logical_or(mine, si * ql >= NQ), 0.0, -1e30).astype(BF)
+    one_b, zero_b = jnp.ones((), BF), jnp.zeros((), BF)
+
+    def two(v, axis):
+        keep = lax.broadcasted_iota(jnp.int32, v.shape, axis) < 64
+        return jnp.concatenate([jnp.where(keep, v, zero_b), jnp.where(keep, zero_b, v)], 1 - axis)
+
+    def diagonal(v):
+        return jnp.concatenate([v[0:64, 0:128], v[64:128, 128:256]], 0)
+
+    def att_tile(qr, kr, qa, ka, kw, cq, ck, cv, keep_e):
+        keys = jnp.concatenate([s.mixed[kr, ck], s.koh[kr, :]], 1)
+        far = s.qoh[:, qr]
+        queries = jnp.concatenate([two(s.qt[:, qa], 0), jnp.concatenate([far, far], 1)], 0)
+        sc = nn(keys, queries)
+        e = jnp.exp2(sc * scale - jnp.max(sc, axis=0, keepdims=True) * scale).astype(BF)
+        keep_e(e)
+        o = nn(jnp.concatenate([s.vt[:, ka], jnp.ones((16, kw), BF)], 0), e)
+        inv = 1.0 / o[128:129, :]
+        s.ctx[qr, cq] = diagonal(o[0:128, :] * inv).T.astype(BF)
+        s.dctx[qr, cq] = diagonal(jnp.broadcast_to(inv, (128, 256))).T.astype(BF)
 
     def pair_cols(hp):
         return at(hp, 128), at(hp + D // 128, 128), at(hp + 2 * D // 128, 128)
@@ -380,22 +409,31 @@
         def _():
             p_copy_out(i - 2, slot).wait()
 
+        cq, ck, cv = pair_cols(hp)
+        whole = rows_at(r * LEN, LEN, LEN)
+        s.qt[...] = s.mixed[whole, cq].T
+        s.vt[...] = s.mixed[whole, cv].T
         for qs, ks, kw, off in TILES:
 
-            def keep_e(h, e):
-                s.pbuf[slot, h, :, off : off + kw] = e
-
-            att_tile(rows_at(r * LEN + qs, 128, 128), rows_at(r * LEN + ks, kw, 128), *pair_cols(hp), keep_e)
+            def keep_e(e):
+                s.pbuf[slot, off : off + kw, :] = e
+
+            qr, kr = rows_at(r * LEN + qs, 128, 128), rows_at(r * LEN + ks, kw, 128)
+            att_tile(qr, kr, slice(qs, qs + 128), slice(ks, ks + kw), kw, cq, ck, cv, keep_e)
         p_copy_out(i, slot).start()
         return 0
 
     lax.fori_loop(0, nrow * (H // 2), att_body, 0)
 
     def att_q_body(hp, _):
-        def keep_e(h, e):
-            s.pq[hp, h] = e
-
-        att_tile(slice(NP, T), slice(NP, T), *pair_cols(hp), keep_e)
+        cq, ck, cv = pair_cols(hp)
+        s.qt[:, 0:NQ] = s.mixed[NP:T, cq].T
+        s.vt[:, 0:NQ] = s.mixed[NP:T, cv].T
+
+        def keep_e(e):
+            s.pq[hp] = e
+
+        att_tile(slice(NP, T), slice(NP, T), slice(0, NQ), slice(0, NQ), NQ, cq, ck, cv, keep_e)
         return 0
 
     lax.fori_loop(0, H // 2, att_q_body, 0)
@@ -430,11 +468,21 @@
 
     lax.fori_loop(0, FF // 256, up_body, 0)
 
+    def remote(src, dst, ssem, rsem, dev):
+        return pltpu.make_async_remote_copy(
+            src_ref=src, dst_ref=dst, send_sem=ssem, recv_sem=rsem, device_id=dev, device_id_type=MESH
+        )
+
     l_wdn.wait()
     l_wpj.wait()
 
+    q_copies = [
+        remote(s.unitb.at[NP:T], s.aq.at[k], s.ss.at[0, k], s.rs.at[0, k], {"psg": lax.rem(me_psg + k, n_psg)})
+        for k in range(1, n_psg)
+    ]
+
     def down_body(t, _):
-        rr = at(t, TT)
+        rr = at(T // TT - 1 - t, TT)
         first = s.y1[rr, :].astype(F32) * v_g1[...] + v_b1[...]
         v = first + (nn(s.hid[rr, :], s.wdn[...]) + v_bdn[...])
         y, inv = norm_stats(v)
@@ -448,6 +496,13 @@
         u = pj * il
         s.unit[rr, :] = u
         s.unitb[rr, :] = u.astype(BF)
+
+        @pl.when(t == 0)
+        def _():
+            pl.semaphore_wait(bar, len(peers))
+            for c in q_copies:
+                c.start()
+
         return 0
 
     lax.fori_loop(0, T // TT, down_body, 0)
@@ -457,22 +512,6 @@
     o_qe = pltpu.make_async_copy(s.unitb.at[NP:T], s.o_qe, s.osem.at[1])
     o_qe.start()
 
-    pl.semaphore_wait(bar, len(peers))
-    sends = []
-
-    def remote(src, dst, ssem, rsem, dev):
-        c = pltpu.make_async_remote_copy(
-            src_ref=src, dst_ref=dst, send_sem=ssem, recv_sem=rsem, device_id=dev, device_id_type=MESH
-        )
-        return c
-
-    q_copies = []
-    for k in range(1, n_psg):
-        c = remote(
-            s.unitb.at[NP:T], s.aq.at[k], s.ss.at[0, k], s.rs.at[0, k], {"psg": lax.rem(me_psg + k, n_psg)}
-        )
-        c.start()
-        q_copies.append(c)
     s.aq[0] = s.unitb[NP:T, :]
 
     for r in range(nrow):
@@ -586,14 +625,7 @@
         rr = slice(m * 256, m * 256 + 256)
         gu = tn(s.gsim[:, rr], aq)
         s.gp[rr, :] = unit_back(gu, rr)
-    for c in g_copies:
-        c.wait_recv()
-    gu = s.own[...]
-    for k in range(1, n_psg):
-        gu = gu + s.qr[k].astype(F32)
-    s.gp[NP:T, :] = unit_back(gu, slice(NP, T))
-
-    s.misc[:, 0:128] = tn(s.gb[...], s.gp[...]).astype(BF)
+    s.vcol[...] = tn(s.gb[0:NP, :], s.gp[0:NP, :])
 
     if sums:
         al = (0, 1, 2, 3)
@@ -605,44 +637,45 @@
             at_step("ff", 3 * z + 2, give_credit, z)
         for z in range(3):
             at_step("ff", 3 * z + 3, take_credit, z)
-        at_step("norm1", 2, ring_d.to_b, 0, 1)
-        at_step("gup", 6, ring_d.to_b, 2, 3)
-        at_step("gout", 0, ring_d.to_z, 0, 1)
-        at_step("gout", 2, ring_d.to_z, 2, 3)
-        at_step("att0", 1, ring_u.to_b, 0, 1)
-        at_step("att0", 1, ring_o.to_a, *al)
-        at_step("att0", 3, ring_u.to_b, 2, 3)
+            at_step("ff", 3 * z + 5, ring_d.to_a, z)
+        at_step("norm1", 0, epoch_wait, 0)
+        at_step("norm1", 0, ring_d.to_b, 0)
+        at_step("norm1", 0, ring_d.to_a, 3)
+        at_step("norm1", 0, give_credit, 4)
+        at_step("norm1", 1, ring_d.to_b, 1)
+        at_step("norm1", 3, ring_d.to_b, 2)
+        at_step("gup", 1, ring_d.to_z, 0, 1)
+        at_step("gup", 3, ring_d.to_b, 3)
+        at_step("gup", 5, start_up)
+        at_step("gup", 7, ring_d.to_z, 2)
+        at_step("dctx", 0, epoch_wait, 1)
+        at_step("dctx", 0, ring_u.to_a, *al)
+        at_step("dctx", 2, ring_d.to_z, 3)
+        at_step("att0", 0, ring_o.to_a, *al)
+        at_step("att0", 2, ring_u.to_b, 0, 1)
+        at_step("att1", 0, ring_1.to_a, *al)
         at_step("att1", 0, ring_d.to_core)
-        at_step("att1", 0, ring_1.to_a, *al)
-        at_step("att1", 1, ring_u.to_z, 0, 1)
-        at_step("att1", 1, ring_o.to_b, *al)
-        at_step("att1", 2, ring_u.to_z, 2, 3)
-        at_step("att1", 2, ring_d.out, put_in(s.o_dn))
-        at_step("att1", 3, ring_o.to_z, *al)
-        at_step("att1", 3, ring_1.to_b, *al)
+        at_step("att1", 1, ring_u.to_b, 2, 3)
+        at_step("att1", 2, ring_u.to_z, 0, 1)
+        at_step("att1", 3, ring_o.to_b, *al)
+        at_step("att1", 3, ring_d.out, put_in(s.o_dn))
         at_step("att2", 0, ring_2.to_a, *al)
-        at_step("att2", 1, ring_1.to_z, *al)
-        at_step("att2", 2, ring_u.to_core)
-        at_step("att2", 2, ring_o.to_core)
-        at_step("att2", 2, ring_2.to_b, *al)
-        at_step("att2", 3, ring_u.out, put_in(s.o_up))
-        at_step("att2", 3, ring_o.out, put_in(s.o_out))
-        at_step("att2", 3, ring_1.to_core)
+        at_step("att2", 1, ring_1.to_b, *al)
+        at_step("att2", 1, ring_u.to_z, 2, 3)
+        at_step("att2", 2, ring_o.to_z, *al)
         at_step("dx", 0, ring_3.to_a, *al)
         at_step("dx", 0, ring_m.to_a, *al)
-        at_step("dx", 0, ring_2.to_z, *al)
-        at_step("dx", 1, ring_1.out, put_group(0))
-        at_step("dx", 2, ring_3.to_b, *al)
-        at_step("dx", 2, ring_m.to_b, *al)
-        at_step("dx", 3, ring_2.to_core)
+        at_step("dx", 0, ring_2.to_b, *al)
+        at_step("dx", 1, ring_1.to_z, *al)
+        at_step("dx", 2, ring_2.to_z, *al)
+        at_step("dx", 3, ring_u.to_core)
 
     s.vr[...] = jnp.zeros_like(s.vr)
 
     def addrow(k, v):
         s.vr[k : k + 1, :] = s.vr[k : k + 1, :] + jnp.sum(v, axis=0, keepdims=True)
 
-    def norm2_body(t, _):
-        rr = at(t, TT)
+    def norm2_rows(rr):
         g = nt(s.gp[rr, :], s.wproj[...])
         y = s.gs[rr, :]
         addrow(6, g * y)
@@ -653,9 +686,20 @@
         b = gs.astype(BF)
         s.gb[rr, :] = b
         addrow(5, b.astype(F32))
-        return 0
-
-    loop('norm2', T // TT, norm2_body)
+
+    def norm2_body(t, _):
+        norm2_rows(at(t, 256))
+        return 0
+
+    loop('norm2', NP // 256, norm2_body)
+    for c in g_copies:
+        c.wait_recv()
+    gu = s.own[...]
+    for k in range(1, n_psg):
+        gu = gu + s.qr[k].astype(F32)
+    s.gp[NP:T, :] = unit_back(gu, slice(NP, T))
+    s.misc[:, 0:128] = (s.vcol[...] + tn(s.gb[NP:T, :], s.gp[NP:T, :])).astype(BF)
+    norm2_rows(slice(NP, T))
 
     def ff_body(n, _):
         c = at(n, 256)
@@ -674,8 +718,6 @@
     if sums:
         epoch_signal(0)
         take_credit(3)
-        epoch_wait(0)
-        ring_d.to_a(*al)
 
     def norm1_body(t, _):
         rr = at(t, TT)
@@ -694,6 +736,8 @@
     loop('norm1', T // TT, norm1_body)
 
     def gup_body(n, _):
+        if sums:
+            n = lax.rem(n + (1 - ring_d.c) * (FF // 512), FF // 256)
         c = at(n, 256)
         s.wup[:, c] = tn(s.fb[...], s.slo[:, c]).astype(BF)
         return 0
@@ -701,8 +745,6 @@
     loop('gup', FF // 256, gup_body)
     if sums:
         epoch_signal(1)
-        epoch_wait(1)
-        ring_u.start(*al)
 
     def dctx_body(t, _):
         rr = at(t, TT)
@@ -710,8 +752,6 @@
         return 0
 
     loop('dctx', T // TT, dctx_body)
-    if sums:
-        ring_u.to_a(*al)
 
     def gout_body(n, _):
         c = at(n, 256)
@@ -720,116 +760,6 @@
 
     loop('gout', D // 256, gout_body)
     if sums:
-        ring_o.start(*al)
-
-    def p_copy_in(j):
-        g, rest = j // (2 * nrow), lax.rem(j, 2 * nrow)
-        i = (rest // 2) * (H // 2) + 2 * g + lax.rem(rest, 2)
-        slot = lax.rem(j, 2)
-        return pltpu.make_async_copy(s.o_p.at[i], s.pbuf.at[slot], s.psem.at[slot])
-
-    steps = nrow * (H // 2)
-    p_copy_in(0).start()
-
-    def back_tile(qr, kr, cq, ck, cv, e_of, keep_ds):
-        do, k, v = s.dctx[qr, cq], s.mixed[kr, ck], s.mixed[kr, cv]
-        prod = (-pltpu.roll(do.astype(F32) * s.ctx[qr, cq].astype(F32), 64, 1)).astype(BF)
-        dq = []
-        for h in range(2):
-            ds = (e_of(h).astype(F32) * nt(mix(h, do, prod), mix(h, v, one_b))).astype(BF)
-            keep_ds(h, ds)
-            dq.append(nn(ds, k))
-        return (mix(0, dq[0], dq[1]) * 0.125).astype(BF)
-
-    def att_back(j, _):
-        g, rest = j // (2 * nrow), lax.rem(j, 2 * nrow)
-        r = rest // 2
-        hp = 2 * g + lax.rem(rest, 2)
-        slot = lax.rem(j, 2)
-
-        @pl.when(j + 1 < steps)
-        def _():
-            p_copy_in(j + 1).start()
-
-        p_copy_in(j).wait()
-        cq, ck, cv = pair_cols(hp)
-        base = r * LEN
-
-        def rws(a, n):
-            return rows_at(base + a, n, 128)
-
-        for qs, ks, kw, off in TILES:
-
-            def keep_ds(h, ds):
-                s.ds[h, :, off : off + kw] = ds
-
-            s.dq[qs : qs + 128, :] = back_tile(
-                rws(qs, 128), rws(ks, kw), cq, ck, cv, lambda h: s.pbuf[slot, h, :, off : off + kw], keep_ds
-            )
-        for kk in range(4):
-            dk = [None, None]
-            dv = [None, None]
-            for h in range(2):
-                for qs, ks, kw, off in TILES:
-                    rel = kk * 128 - ks
-                    if rel < 0 or rel >= kw:
-                        continue
-                    qt = s.mixed[rws(qs, 128), cq]
-                    ot = s.dctx[rws(qs, 128), cq]
-                    a = tn(s.ds[h, :, off + rel : off + rel + 128], qt)
-                    b = tn(s.pbuf[slot, h, :, off + rel : off + rel + 128], ot)
-                    dk[h] = a if dk[h] is None else dk[h] + a
-                    dv[h] = b if dv[h] is None else dv[h] + b
-            s.dk[kk * 128 : kk * 128 + 128, :] = (mix(0, dk[0], dk[1]) * 0.125).astype(BF)
-            s.dv[kk * 128 : kk * 128 + 128, :] = mix(0, dv[0], dv[1]).astype(BF)
-        s.mixed[rws(0, LEN), cq] = s.dq[...]
-        s.mixed[rws(0, LEN), ck] = s.dk[...]
-        s.mixed[rws(0, LEN), cv] = s.dv[...]
-        return 0
-
-    def att_back_q(hp, _):
-        cq, ck, cv = pair_cols(hp)
-        rr = slice(NP, T)
-        q, do = s.mixed[rr, cq], s.dctx[rr, cq]
-        grads = [None, None]
-
-        def keep_ds(h, ds):
-            grads[h] = ds
-
-        dq = back_tile(rr, rr, cq, ck, cv, lambda h: s.pq[hp, h], keep_ds)
-        dk = [tn(grads[h], q) for h in range(2)]
-        dv = [tn(s.pq[hp, h], do) for h in range(2)]
-        s.mixed[rr, cq] = dq
-        s.mixed[rr, ck] = (mix(0, dk[0], dk[1]) * 0.125).astype(BF)
-        s.mixed[rr, cv] = mix(0, dv[0], dv[1]).astype(BF)
-        return 0
-
-    lax.fori_loop(0, H // 2, att_back_q, 0)
-
-    groups = (s.fb, s.gb, s.ctx)
-
-    def group_grad(g):
-        for w in range(3):
-            c = w * D + g * 256
-            groups[g][0:D, w * 256 : w * 256 + 256] = tn(s.x[...], s.mixed[:, c : c + 256]).astype(BF)
-
-    for g in range(3):
-
-        @functools.partial(loop, 'att%d' % g, 2 * nrow)
-        def _(j, _, g=g):
-            att_back(2 * nrow * g + j, 0)
-
-        group_grad(g)
-        if sums:
-            (ring_1, ring_2, ring_3)[g].start(*al)
-    for w, k in ((0, 0), (2, 1)):
-        s.vr[k : k + 1, :] = jnp.sum(s.mixed[:, w * D : w * D + D].astype(F32), axis=0, keepdims=True)
-
-    if sums:
-        pad = jnp.zeros((120, 128), F32)
-        for i in range(D // 128):
-            v = s.vr[:, i * 128 : i * 128 + 128]
-            s.vcol[i * 128 : i * 128 + 128, :] = jnp.concatenate([v, pad], 0).T
         q = D // 32
         lane = lax.broadcasted_iota(jnp.int32, (q, 128), 1)
         for i in range(FF // 384):
@@ -837,11 +767,107 @@
                 v = s.bup[0:1, i * 384 + k * 128 : i * 384 + k * 128 + 128]
                 s.tcol[k * 128 : k * 128 + 128, :] = jnp.broadcast_to(v, (128, 128)).T
             for d in range(4):
-                rr = slice((4 * i + d) * q, (4 * i + d) * q + q)
-                v = s.vcol[rr, :]
+                v = jnp.zeros((q, 128), F32)
                 for k in range(4):
                     v = jnp.where(lane == 8 + k, s.tcol[(4 * d + k) * q : (4 * d + k) * q + q, :], v)
-                s.vcol[rr, :] = v
+                s.vcol[(4 * i + d) * q : (4 * i + d) * q + q, :] = v
+    if sums:
+        ring_o.start(*al)
+
+    def p_copy_in(j):
+        g, rest = j // (2 * nrow), lax.rem(j, 2 * nrow)
+        i = (rest // 2) * (H // 2) + 2 * g + lax.rem(rest, 2)
+        slot = lax.rem(j, 2)
+        return pltpu.make_async_copy(s.o_p.at[i], s.pbuf.at[slot], s.psem.at[slot])
+
+    steps = nrow * (H // 2)
+    p_copy_in(0).start()
+
+    def turn(rr, n, cq, ck):
+        do = s.dctx[rr, cq]
+        s.qt[:, 0:n] = do.T
+        s.vt[:, 0:n] = (-do.astype(F32) * s.ctx[rr, cq].astype(F32)).astype(BF).T
+        s.kt[:, 0:n] = s.mixed[rr, ck].T
+
+    def back_tile(qr, kr, qa, ka, kw, cq, ck, cv, e):
+        values = jnp.concatenate([s.mixed[kr, cv], jnp.ones((kw, 128), BF)], 1)
+        grads = jnp.concatenate([two(s.qt[:, qa], 0), two(s.vt[:, qa], 0)], 0)
+        ds = (e.astype(F32) * nn(values, grads)).astype(BF)
+        dk = nn(ds, two(s.mixed[qr, cq], 1))
+        dv = nn(e, two(s.dctx[qr, cq], 1))
+        dq = (diagonal(nn(s.kt[:, ka], ds)).T * 0.125).astype(BF)
+        return dq, dk, dv
+
+    def att_back(j, _):
+        g, rest = j // (2 * nrow), lax.rem(j, 2 * nrow)
+        r = rest // 2
+        hp = 2 * g + lax.rem(rest, 2)
+        slot = lax.rem(j, 2)
+
+        @pl.when(j + 1 < steps)
+        def _():
+            p_copy_in(j + 1).start()
+
+        p_copy_in(j).wait()
+        cq, ck, cv = pair_cols(hp)
+        base = r * LEN
+
+        def rws(a, n):
+            return rows_at(base + a, n, 128)
+
+        turn(rws(0, LEN), LEN, cq, ck)
+        s.dka[...] = jnp.zeros_like(s.dka)
+        s.dva[...] = jnp.zeros_like(s.dva)
+        for qs, ks, kw, off in TILES:
+            dq, dk, dv = back_tile(
+                rws(qs, 128), rws(ks, kw), slice(qs, qs + 128), slice(ks, ks + kw), kw, cq, ck, cv,
+                s.pbuf[slot, off : off + kw, :],
+            )
+            s.dq[qs : qs + 128, :] = dq
+            s.dka[ks : ks + kw, :] += dk
+            s.dva[ks : ks + kw, :] += dv
+        s.mixed[rws(0, LEN), cq] = s.dq[...]
+        s.mixed[rws(0, LEN), ck] = (s.dka[...] * 0.125).astype(BF)
+        s.mixed[rws(0, LEN), cv] = s.dva[...].astype(BF)
+        return 0
+
+    def att_back_q(hp, _):
+        cq, ck, cv = pair_cols(hp)
+        rr = slice(NP, T)
+        turn(rr, NQ, cq, ck)
+        dq, dk, dv = back_tile(rr, rr, slice(0, NQ), slice(0, NQ), NQ, cq, ck, cv, s.pq[hp])
+        s.mixed[rr, cq] = dq
+        s.mixed[rr, ck] = (dk * 0.125).astype(BF)
+        s.mixed[rr, cv] = dv.astype(BF)
+        return 0
+
+    lax.fori_loop(0, H // 2, att_back_q, 0)
+
+    groups = (s.fb, s.gb, s.ctx)
+
+    def group_grad(g):
+        for w in range(3):
+            c = w * D + g * 256
+            groups[g][0:D, w * 256 : w * 256 + 256] = tn(s.x[...], s.mixed[:, c : c + 256]).astype(BF)
+
+    for g in range(3):
+
+        @functools.partial(loop, 'att%d' % g, 2 * nrow)
+        def _(j, _, g=g):
+            att_back(2 * nrow * g + j, 0)
+
+        group_grad(g)
+        if sums:
+            (ring_1, ring_2, ring_3)[g].start(*al)
+    for w, k in ((0, 0), (2, 1)):
+        s.vr[k : k + 1, :] = jnp.sum(s.mixed[:, w * D : w * D + D].astype(F32), axis=0, keepdims=True)
+
+    if sums:
+        pad = jnp.zeros((120, 128), F32)
+        few = lax.broadcasted_iota(jnp.int32, (128, 128), 1) < 8
+        for i in range(D // 128):
+            rr = slice(i * 128, i * 128 + 128)
+            s.vcol[rr, :] = jnp.where(few, jnp.concatenate([s.vr[:, rr], pad], 0).T, s.vcol[rr, :])
         s.misc[:, 128:256] = s.vcol[...].astype(BF)
         ring_m.start(*al)
 
@@ -870,8 +896,16 @@
     for c in outs:
         c.start()
     if sums:
+        ring_3.to_b(*al)
+        ring_m.to_b(*al)
+        ring_o.to_core()
+        ring_u.out(put_in(s.o_up))
+        ring_1.to_core()
+        ring_o.out(put_in(s.o_out))
         ring_3.to_z(*al)
         ring_m.to_z(*al)
+        ring_2.to_core()
+        ring_1.out(put_group(0))
         ring_2.out(put_group(1))
         ring_3.to_core()
         ring_m.to_core()
@@ -998,7 +1032,7 @@
             ("o_loss", sd((8, 128), F32), vm),
             ("o_gp", sd((NP, D), F32), any_spec),
             ("o_gq", sd((NQ, D), F32), any_spec),
-            ("o_p", sd((npair, 2, 128, PW), BF), any_spec),
+            ("o_p", sd((npair, PW, 256), BF), any_spec),
         ]
         n_dev = n_dp * n_psg
         if cfg.sums:
@@ -1032,10 +1066,13 @@
             ("vin", V((8, D), F32)),
             ("tsq", V((128, 128), F32)),
             ("mixed", V((T, 3 * D), BF)),
-            ("pbuf", V((2, 2, 128, PW), BF)),
-            ("pq", V((H // 2, 2, NQ, NQ), BF)),
+            ("pbuf", V((2, PW, 256), BF)),
+            ("pq", V((H // 2, NQ, 256), BF)),
             ("koh", V((T, 128), BF)),
-            ("qoh", V((T, 128), BF)),
+            ("qoh", V((128, T), BF)),
+            ("qt", V((128, LEN), BF)),
+            ("vt", V((128, LEN), BF)),
+            ("kt", V((128, LEN), BF)),
             ("ctx", V((T, D), BF)),
             ("y1", V((T, D), BF)),
             ("fb", V((T, D), BF)),
@@ -1063,10 +1100,9 @@
             ("vcol", V((D, 128), F32)),
             ("bup", V((8, FF), F32)),
             ("dctx", V((T, D), BF)),
-            ("ds", V((2, 128, PW), BF)),
             ("dq", V((LEN, 128), BF)),
-            ("dk", V((LEN, 128), BF)),
-            ("dv", V((LEN, 128), BF)),
+            ("dka", V((LEN, 128), F32)),
+            ("dva", V((LEN, 128), F32)),
             ("lsem", DMA((7,))),
             ("psem", DMA((2,))),
             ("osem", DMA((11,))),
@@ -1090,7 +1126,8 @@
                 ("rm", V((b // 2, 128), F32)),
                 ("gss", DMA((7, 18))),
                 ("grs", DMA((7, 18))),
-                ("credit", pltpu.SemaphoreType.REGULAR((4,))),
+                ("arecv", V((8 * e, D // 2), BF)),
+                ("credit", pltpu.SemaphoreType.REGULAR((5,))),
                 ("epoch", pltpu.SemaphoreType.REGULAR((2,))),
             ]
         cfg.names = [a for a, *_ in ins] + [a for a, *_ in outs] + [a for a, _ in scratch]

time: 198 us -> 176 us (0.89)
  Pallas kernels: 197 us -> 175 us
    pallas_call x1, Pallas kernels: 192 us -> 170 us  [body(): pl.pallas_call(functools.partial(kernel, cfg), out_shape=[o[1] for o in o...]
where the time goes in v3:
time: 176 us
  Pallas kernels  175 us (99%)
    pallas_call x1, Pallas kernels, body(): pl.pallas_call(functools.partial(kernel, cfg), out_shape=[o[1] for o in o...  170 us
    pallas_call x1, Pallas kernels, finish(): pl.pallas_call(functools.partial(finish_kernel, all_names), out_shape=[v[...  5.42 us

profile of v3, /device:TPU:1, one launch (start us, length us, event | category | flops | bytes accessed | tf_op | source)
XLA Modules:
  0.0 176.1 jit_solution(16201673332818427870)
XLA Ops:
  0.7 169.9 %shard_map.321 = (bf16[1024,128]{1,0:T(8,128)(2,1)}, bf16[128,128]{1,0:T(8,128)(2,1)}, f32[8,128]{1,0:T(8,128)}, f32[1024,768]{1,0:T(8,128)}, f32[128,768]{1,0:T...) custom-call(bf16[1024,768]{1,0:T(8,128)(2,1)} %bitcast.7, ...), custom_call_target="tpu_custom_call" | custom-call | tf_op jit(solution)/shard_map/pallas_call | solution.py:1134
  170.5 5.4 %shard_map.322 = (bf16[1024,128]{1,0:T(8,128)(2,1)}, bf16[128,128]{1,0:T(8,128)(2,1)}, f32[1024,768]{1,0:T(8,128)}, f32[128,768]{1,0:T(8,128)}, f32[96,768]{1,0:...) custom-call(bf16[1024,128]{1,0:T(8,128)(2,1)} %get-tuple-element.48., ...), custom_call_target="tpu_custom_call" | custom-call | tf_op jit(solution)/shard_map/pallas_call | solution.py:977

commit v4 on v3

--- a/solution.py
+++ b/solution.py
@@ -52,8 +52,9 @@
 
 
 class Ring:
-    def __init__(self, s, u, g, b, half, places, f, rd, where):
+    def __init__(self, s, u, g, b, half, places, f, rd, where, stride=None, off=0):
         self.s, self.u, self.g, self.b, self.half = s, u, g, b, half
+        self.stride, self.off = stride or half, off
         self.c_at, self.a_at, self.b_at, self.z_at = places
         self.f, self.rd = f, rd
         dp, psg = where
@@ -64,7 +65,7 @@
         self.zn = [{"dp": lax.rem(self.z + k, 4) * 2 + self.x} for k in range(1, 4)]
 
     def cols(self, c):
-        return pl.ds(pl.multiple_of(c * self.half, 128), self.half)
+        return pl.ds(pl.multiple_of(c * self.stride + self.off, 128), self.half)
 
     def part(self, row, n, c):
         return self.g.at[pl.ds(pl.multiple_of(row * self.b, 16), n * self.b), self.cols(c)]
@@ -198,11 +199,12 @@
         place(s.hid, lambda z: (e * z, 6 * h), e, h),
         place(s.hid, lambda z: (e * z, 7 * h), e, h),
     )
-    up = (
-        place(s.hid, lambda z: (4 * b * z, 0), 4 * b, w),
-        place(s.slo, lambda z: (2 * b * z, w), b, w),
-        place(s.slo, lambda z: (b * (8 + z), w), b, w),
-        place(s.slo, lambda z: (b * (12 + z), w), b, w),
+    v = w // 2
+    ups = lambda k: (
+        place(s.hid, lambda z: (4 * b * z, k * v), 4 * b, v),
+        place(s.hid, lambda z: (b * (8 * k + 2 * z), 2 * v), b, v),
+        place(s.slo, lambda z: (b * z, k * v), b, v),
+        place(s.slo, lambda z: (b * (4 + z), k * v), b, v),
     )
     second = (
         place(s.y1, lambda z: (4 * b * z, 0), 4 * b, h),
@@ -225,7 +227,10 @@
     mk = lambda u, g, bb, half, places, f, rd: Ring(s, u, g, bb, half, places, f, rd, where)
     return (
         mk(0, s.wdn, e, h, down, s.fd, s.rd),
-        mk(1, s.wup, b, w, up, s.fu, s.ru),
+        (
+            Ring(s, 1, s.wup, b, v, ups(0), s.fu.at[0], s.ru.at[0], where, w, 0),
+            Ring(s, 7, s.wup, b, v, ups(1), s.fu.at[1], s.ru.at[1], where, w, v),
+        ),
         mk(2, s.wout, b, h, spots(s.hid, 0), s.fq.at[0], s.rq.at[0]),
         mk(3, s.fb, b, h, spots(s.slo, 0), s.fq.at[1], s.rq.at[1]),
         mk(4, s.gb, b, h, second, s.fq.at[2], s.rq.at[2]),
@@ -274,7 +279,8 @@
 
     sums = cfg.sums
     if sums:
-        ring_d, ring_u, ring_o, ring_1, ring_2, ring_3, ring_m = rings = make_rings(s, cfg, (me_dp, me_psg))
+        ring_d, (ring_u, ring_v), ring_o, ring_1, ring_2, ring_3, ring_m = make_rings(s, cfg, (me_dp, me_psg))
+        rings = (ring_d, ring_u, ring_v, ring_o, ring_1, ring_2, ring_3, ring_m)
 
         def epoch_signal(k):
             for dev in [ring_d.core, ring_d.xn, ring_d.yn] + ring_d.zn:
@@ -315,6 +321,13 @@
     def put_in(ref):
         def put(c, v):
             ref[:, pl.ds(pl.multiple_of(c * v.shape[1], 128), v.shape[1])] = v
+
+        return put
+
+    def put_up(k):
+        def put(c, v):
+            n = v.shape[1]
+            s.o_up[:, pl.ds(pl.multiple_of((2 * c + k) * n, 128), n)] = v
 
         return put
 
@@ -444,7 +457,7 @@
     l_wout.wait()
 
     def out_body(t, _):
-        rr = at(t, TT)
+        rr = at(t, T // 2)
         v = nn(s.ctx[rr, :], s.wout[...]) + v_bout[...] + s.x[rr, :].astype(F32)
         y, inv = norm_stats(v)
         s.y1[rr, :] = y.astype(BF)
@@ -452,14 +465,13 @@
         s.fb[rr, :] = (y * v_g1[...] + v_b1[...]).astype(BF)
         return 0
 
-    lax.fori_loop(0, T // TT, out_body, 0)
+    lax.fori_loop(0, 2, out_body, 0)
 
     l_wup.wait()
 
     def up_body(n, _):
         c = at(n, 256)
-        for m in range(T // TT):
-            rr = slice(m * TT, m * TT + TT)
+        for rr in (slice(0, T),):
             h = nn(s.fb[rr, :], s.wup[:, c]) + s.bup[0:1, c]
             cdf = 0.5 * (1.0 + lax.erf(h * 0.7071067811865476))
             s.hid[rr, c] = (h * cdf).astype(BF)
@@ -482,7 +494,7 @@
     ]
 
     def down_body(t, _):
-        rr = at(T // TT - 1 - t, TT)
+        rr = at(1 - t, T // 2)
         first = s.y1[rr, :].astype(F32) * v_g1[...] + v_b1[...]
         v = first + (nn(s.hid[rr, :], s.wdn[...]) + v_bdn[...])
         y, inv = norm_stats(v)
@@ -505,7 +517,7 @@
 
         return 0
 
-    lax.fori_loop(0, T // TT, down_body, 0)
+    lax.fori_loop(0, 2, down_body, 0)
 
     o_pe = pltpu.make_async_copy(s.unitb.at[0:NP], s.o_pe, s.osem.at[0])
     o_pe.start()
@@ -643,32 +655,38 @@
         at_step("norm1", 0, ring_d.to_a, 3)
         at_step("norm1", 0, give_credit, 4)
         at_step("norm1", 1, ring_d.to_b, 1)
-        at_step("norm1", 3, ring_d.to_b, 2)
-        at_step("gup", 1, ring_d.to_z, 0, 1)
-        at_step("gup", 3, ring_d.to_b, 3)
-        at_step("gup", 5, start_up)
-        at_step("gup", 7, ring_d.to_z, 2)
+        at_step("gup", 1, ring_d.to_b, 2)
+        at_step("gup", 2, start_up)
+        at_step("gup", 4, ring_d.to_z, 1)
+        at_step("gup", 6, ring_u.to_a, *al)
+        at_step("gup", 8, ring_v.start, *al)
+        at_step("gup", 11, ring_d.to_b, 3)
         at_step("dctx", 0, epoch_wait, 1)
-        at_step("dctx", 0, ring_u.to_a, *al)
-        at_step("dctx", 2, ring_d.to_z, 3)
-        at_step("att0", 0, ring_o.to_a, *al)
-        at_step("att0", 2, ring_u.to_b, 0, 1)
+        at_step("dctx", 0, ring_d.to_z, 0)
+        at_step("dctx", 2, ring_d.to_z, 2)
+        at_step("gout", 0, ring_v.to_a, *al)
+        at_step("att0", 0, ring_d.to_z, 3)
+        at_step("att0", 0, ring_u.to_b, *al)
+        at_step("att0", 1, ring_o.to_a, *al)
+        at_step("att1", 0, ring_v.to_b, *al)
         at_step("att1", 0, ring_1.to_a, *al)
-        at_step("att1", 0, ring_d.to_core)
-        at_step("att1", 1, ring_u.to_b, 2, 3)
-        at_step("att1", 2, ring_u.to_z, 0, 1)
-        at_step("att1", 3, ring_o.to_b, *al)
-        at_step("att1", 3, ring_d.out, put_in(s.o_dn))
+        at_step("att1", 0, ring_u.to_z, *al)
+        at_step("att1", 1, ring_d.to_core)
+        at_step("att1", 2, ring_o.to_b, *al)
         at_step("att2", 0, ring_2.to_a, *al)
+        at_step("att2", 0, ring_v.to_z, *al)
+        at_step("att2", 0, ring_d.out, put_in(s.o_dn))
         at_step("att2", 1, ring_1.to_b, *al)
-        at_step("att2", 1, ring_u.to_z, 2, 3)
         at_step("att2", 2, ring_o.to_z, *al)
+        at_step("att2", 3, ring_u.to_core)
         at_step("dx", 0, ring_3.to_a, *al)
         at_step("dx", 0, ring_m.to_a, *al)
         at_step("dx", 0, ring_2.to_b, *al)
-        at_step("dx", 1, ring_1.to_z, *al)
+        at_step("dx", 0, ring_1.to_z, *al)
+        at_step("dx", 1, ring_u.out, put_up(0))
+        at_step("dx", 2, ring_v.to_core)
         at_step("dx", 2, ring_2.to_z, *al)
-        at_step("dx", 3, ring_u.to_core)
+        at_step("dx", 3, ring_o.to_core)
 
     s.vr[...] = jnp.zeros_like(s.vr)
 
@@ -737,7 +755,9 @@
 
     def gup_body(n, _):
         if sums:
-            n = lax.rem(n + (1 - ring_d.c) * (FF // 512), FF // 256)
+            q = FF // 1024
+            turn, k = n // q, lax.rem(n, q)
+            n = lax.rem(1 - ring_d.c + turn, 2) * 2 * q + (turn // 2) * q + k
         c = at(n, 256)
         s.wup[:, c] = tn(s.fb[...], s.slo[:, c]).astype(BF)
         return 0
@@ -898,8 +918,7 @@
     if sums:
         ring_3.to_b(*al)
         ring_m.to_b(*al)
-        ring_o.to_core()
-        ring_u.out(put_in(s.o_up))
+        ring_v.out(put_up(1))
         ring_1.to_core()
         ring_o.out(put_in(s.o_out))
         ring_3.to_z(*al)
@@ -1118,14 +1137,14 @@
                 ("mrecv", V((31 * b, 128), BF)),
                 ("fd", V((e, D // 2), F32)),
                 ("rd", V((e // 2, D // 2), F32)),
-                ("fu", V((b, FF // 2), F32)),
-                ("ru", V((b // 2, FF // 2), F32)),
+                ("fu", V((2, b, FF // 4), F32)),
+                ("ru", V((2, b // 2, FF // 4), F32)),
                 ("fq", V((4, b, D // 2), F32)),
                 ("rq", V((4, b // 2, D // 2), F32)),
                 ("fm", V((b, 128), F32)),
                 ("rm", V((b // 2, 128), F32)),
-                ("gss", DMA((7, 18))),
-                ("grs", DMA((7, 18))),
+                ("gss", DMA((8, 18))),
+                ("grs", DMA((8, 18))),
                 ("arecv", V((8 * e, D // 2), BF)),
                 ("credit", pltpu.SemaphoreType.REGULAR((5,))),
                 ("epoch", pltpu.SemaphoreType.REGULAR((2,))),

time: 176 us -> 166 us (0.943)
  Pallas kernels: 175 us -> 165 us
    pallas_call x1, Pallas kernels: 170 us -> 159 us  [body(): pl.pallas_call(functools.partial(kernel, cfg), out_shape=[o[1] for o in o...]
where the time goes in v4:
time: 166 us
  Pallas kernels  165 us (99%)
    pallas_call x1, Pallas kernels, body(): pl.pallas_call(functools.partial(kernel, cfg), out_shape=[o[1] for o in o...  159 us
    pallas_call x1, Pallas kernels, finish(): pl.pallas_call(functools.partial(finish_kernel, all_names), out_shape=[v[...  5.42 us

profile of v4, /device:TPU:1, one launch (start us, length us, event | category | flops | bytes accessed | tf_op | source)
XLA Modules:
  0.0 165.8 jit_solution(17560290057494935254)
XLA Ops:
  0.7 159.5 %shard_map.321 = (bf16[1024,128]{1,0:T(8,128)(2,1)}, bf16[128,128]{1,0:T(8,128)(2,1)}, f32[8,128]{1,0:T(8,128)}, f32[1024,768]{1,0:T(8,128)}, f32[128,768]{1,0:T...) custom-call(bf16[1024,768]{1,0:T(8,128)(2,1)} %bitcast.7, ...), custom_call_target="tpu_custom_call" | custom-call | tf_op jit(solution)/shard_map/pallas_call | solution.py:1153
  160.2 5.4 %shard_map.322 = (bf16[1024,128]{1,0:T(8,128)(2,1)}, bf16[128,128]{1,0:T(8,128)(2,1)}, f32[1024,768]{1,0:T(8,128)}, f32[128,768]{1,0:T(8,128)}, f32[96,768]{1,0:...) custom-call(bf16[1024,128]{1,0:T(8,128)(2,1)} %get-tuple-element.48., ...), custom_call_target="tpu_custom_call" | custom-call | tf_op jit(solution)/shard_map/pallas_call | solution.py:996

commit v5 on v4

--- a/solution.py
+++ b/solution.py
@@ -679,8 +679,6 @@
         at_step("att2", 1, ring_1.to_b, *al)
         at_step("att2", 2, ring_o.to_z, *al)
         at_step("att2", 3, ring_u.to_core)
-        at_step("dx", 0, ring_3.to_a, *al)
-        at_step("dx", 0, ring_m.to_a, *al)
         at_step("dx", 0, ring_2.to_b, *al)
         at_step("dx", 0, ring_1.to_z, *al)
         at_step("dx", 1, ring_u.out, put_up(0))
@@ -890,6 +888,8 @@
             s.vcol[rr, :] = jnp.where(few, jnp.concatenate([s.vr[:, rr], pad], 0).T, s.vcol[rr, :])
         s.misc[:, 128:256] = s.vcol[...].astype(BF)
         ring_m.start(*al)
+        ring_3.to_a(*al)
+        ring_m.to_a(*al)
 
     def dx_body(t, _):
         rr = at(t, TT)

time: 166 us -> 165 us (level)
  no operation moved by 1% of the time
where the time goes in v5:
time: 165 us; the launch traced here: 164 us
  Pallas kernels  164 us (99%)
    pallas_call x1, Pallas kernels, body(): pl.pallas_call(functools.partial(kernel, cfg), out_shape=[o[1] for o in o...  158 us
    pallas_call x1, Pallas kernels, finish(): pl.pallas_call(functools.partial(finish_kernel, all_names), out_shape=[v[...  5.42 us

profile of v5, /device:TPU:1, one launch (start us, length us, event | category | flops | bytes accessed | tf_op | source)
XLA Modules:
  0.0 164.4 jit_solution(12816757583077142052)
XLA Ops:
  0.7 158.1 %shard_map.321 = (bf16[1024,128]{1,0:T(8,128)(2,1)}, bf16[128,128]{1,0:T(8,128)(2,1)}, f32[8,128]{1,0:T(8,128)}, f32[1024,768]{1,0:T(8,128)}, f32[128,768]{1,0:T...) custom-call(bf16[1024,768]{1,0:T(8,128)(2,1)} %bitcast.7, ...), custom_call_target="tpu_custom_call" | custom-call | tf_op jit(solution)/shard_map/pallas_call | solution.py:1153
  158.8 5.4 %shard_map.322 = (bf16[1024,128]{1,0:T(8,128)(2,1)}, bf16[128,128]{1,0:T(8,128)(2,1)}, f32[1024,768]{1,0:T(8,128)}, f32[128,768]{1,0:T(8,128)}, f32[96,768]{1,0:...) custom-call(bf16[1024,128]{1,0:T(8,128)(2,1)} %get-tuple-element.48., ...), custom_call_target="tpu_custom_call" | custom-call | tf_op jit(solution)/shard_map/pallas_call | solution.py:996
